TPU v7x, 32 devices: a whole 2x2x4 slice. The times are simulated.
32 devices in a mesh: dp: 16 (over z, y, x), tensor: 2 (over core).
Axes of the slice: x: 2, y: 2, z: 4, core: 2. Of those that a mesh axis runs over, the one named last changes fastest.
Arguments:
- clips: bfloat16 [16, 1569, 768], P('dp'), may hold values from -6 to 6
- cotangent: bfloat16 [16, 1569, 768], P('dp'), may hold values from -6 to 6
- live: int32 [16], P('dp'), may hold values 0 or 1
- time_gain: float32 [768], replicated, may hold values from 0.25 to 1.75
- time_shift: float32 [768], replicated, may hold values from -3 to 3
- time_inproj: bfloat16 [768, 3, 768], P(None, None, 'tensor'), may hold values from -0.21875 to 0.21875
- time_inbias: float32 [2, 768], P(None, 'tensor'), may hold values from -3 to 3
- time_outproj: bfloat16 [768, 768], P('tensor'), may hold values from -0.625 to 0.625
- time_outbias: float32 [768], replicated, may hold values from -3 to 3
- time_mixer: bfloat16 [768, 768], P('tensor'), may hold values from -0.21875 to 0.21875
- time_mixbias: float32 [768], replicated, may hold values from -3 to 3
- space_gain: float32 [768], replicated, may hold values from 0.25 to 1.75
- space_shift: float32 [768], replicated, may hold values from -3 to 3
- space_inproj: bfloat16 [768, 3, 768], P(None, None, 'tensor'), may hold values from -0.21875 to 0.21875
- space_inbias: float32 [2, 768], P(None, 'tensor'), may hold values from -3 to 3
- space_outproj: bfloat16 [768, 768], P('tensor'), may hold values from -1.75 to 1.75
- space_outbias: float32 [768], replicated, may hold values from -4 to 4
- feed_gain: float32 [768], replicated, may hold values from 0.25 to 1.75
- feed_shift: float32 [768], replicated, may hold values from -3 to 3
- feed_upward: bfloat16 [768, 3072], P(None, 'tensor'), may hold values from -0.21875 to 0.21875
- feed_upbias: float32 [3072], P('tensor'), may hold values from -3 to 3
- feed_down: bfloat16 [3072, 768], P('tensor'), may hold values from -0.15625 to 0.15625
- feed_downbias: float32 [768], replicated, may hold values from -4 to 4
Outputs:
- mixed: bfloat16 [16, 1569, 768], P('dp')
- grad_clips: bfloat16 [16, 1569, 768], P('dp')
- grad_time_gain: float32 [768], P('dp')
- grad_time_shift: float32 [768], P('dp')
- grad_time_inproj: float32 [768, 3, 768], P('dp', None, 'tensor')
- grad_time_inbias: float32 [2, 768], P(None, ('tensor', 'dp'))
- grad_time_outproj: float32 [768, 768], P('tensor', 'dp')
- grad_time_outbias: float32 [768], P('dp')
- grad_time_mixer: float32 [768, 768], P('tensor', 'dp')
- grad_time_mixbias: float32 [768], P('dp')
- grad_space_gain: float32 [768], P('dp')
- grad_space_shift: float32 [768], P('dp')
- grad_space_inproj: float32 [768, 3, 768], P('dp', None, 'tensor')
- grad_space_inbias: float32 [2, 768], P(None, ('tensor', 'dp'))
- grad_space_outproj: float32 [768, 768], P('tensor', 'dp')
- grad_space_outbias: float32 [768], P('dp')
- grad_feed_gain: float32 [768], P('dp')
- grad_feed_shift: float32 [768], P('dp')
- grad_feed_upward: float32 [768, 3072], P('dp', 'tensor')
- grad_feed_upbias: float32 [3072], P(('tensor', 'dp'))
- grad_feed_down: float32 [3072, 768], P('tensor', 'dp')
- grad_feed_downbias: float32 [768], P('dp')
Inputs may be any that keep to these rules, and one draw needn't show every extreme that they name: `live`: 1 where the data group holds a clip, 0 where its slot is empty.
All inputs are finite; a program needn't handle non-finite values.
Results may differ from a plain program's by a relative error of at most 0.03.
Values may be sent and summed in bfloat16 or wider, within the bound.
No kernel may reach another device: no remote copies, remote signals or barrier semaphores. Data moves between devices by JAX's collectives and lax.ppermute only.
A program may use at most 256 MiB of HBM per device.

v0:
```python
import jax
import jax.numpy as jnp
from jax import lax
from jax.sharding import PartitionSpec as P

HEAD = 64
FRAMES = 8
PLACES = 196


def layer_norm(field, gain, shift):
    center = field - jnp.mean(field, axis=-1, keepdims=True)
    spread_sq = jnp.mean(center * center, axis=-1, keepdims=True)
    return center * lax.rsqrt(spread_sq + 1e-06) * gain + shift


def norm_back(field, gain, shift, grad):
    _, pull = jax.vjp(layer_norm, field, gain, shift)
    return pull(grad)


def heads_of(field):
    return field.reshape(field.shape[:-1] + (field.shape[-1] // HEAD, HEAD))


def merge_heads(field):
    return field.reshape(field.shape[:-2] + (field.shape[-2] * field.shape[-1],))


def branch_total(terms):
    half_sum = lax.psum_scatter(terms, "tensor", scatter_dimension=1, tiled=True)
    return lax.all_gather(half_sum, "tensor", axis=1, tiled=True)


def input_total(terms):
    half_sum = lax.psum_scatter(terms, "tensor", scatter_dimension=1, tiled=True)
    return lax.all_gather(half_sum, "tensor", axis=1, tiled=True)


def project_heads(normed, inproj, inbias, scale):
    linear = jnp.einsum("bld,dck->cblk", normed, inproj, preferred_element_type=jnp.float32)
    query = ((linear[0] + inbias[0]) * scale).astype(jnp.bfloat16)
    keys = linear[1].astype(jnp.bfloat16)
    values = (linear[2] + inbias[1]).astype(jnp.bfloat16)
    return (heads_of(query), heads_of(keys), heads_of(values))


def attend_forward(query, keys, values):
    scores = jnp.einsum("bihe,bjhe->bhij", query, keys, preferred_element_type=jnp.float32)
    peak = jnp.max(scores, axis=-1, keepdims=True)
    expon = jnp.exp(scores - peak)
    totals = jnp.sum(expon, axis=-1, keepdims=True)
    logsum = peak + jnp.log(totals)
    probs = (expon / totals).astype(jnp.bfloat16)
    mixed = jnp.einsum("bhij,bjhe->bihe", probs, values, preferred_element_type=jnp.float32)
    return (mixed.astype(jnp.bfloat16), logsum)


def attend_backward(query, keys, values, logsum, d_mixed):
    scores = jnp.einsum("bihe,bjhe->bhij", query, keys, preferred_element_type=jnp.float32)
    probs = jnp.exp(scores - logsum)
    d_values = jnp.einsum(
        "bhij,bihe->bjhe", probs.astype(jnp.bfloat16), d_mixed, preferred_element_type=jnp.float32
    )
    d_probs = jnp.einsum("bihe,bjhe->bhij", d_mixed, values, preferred_element_type=jnp.float32)
    inner = jnp.sum(probs * d_probs, axis=-1, keepdims=True)
    d_scores = (probs * (d_probs - inner)).astype(jnp.bfloat16)
    d_query = jnp.einsum("bhij,bjhe->bihe", d_scores, keys, preferred_element_type=jnp.float32)
    d_keys = jnp.einsum("bhij,bihe->bjhe", d_scores, query, preferred_element_type=jnp.float32)
    return (d_query, d_keys, d_values)


def inproj_back(d_query, d_keys, d_values, normed, inproj, scale):
    query_low = merge_heads(d_query).astype(jnp.bfloat16) * scale
    keys_low = merge_heads(d_keys).astype(jnp.bfloat16)
    values_low = merge_heads(d_values).astype(jnp.bfloat16)
    stacked = jnp.stack([query_low, keys_low, values_low])
    grad_inproj = jnp.einsum("bld,cblk->dck", normed, stacked, preferred_element_type=jnp.float32)
    grad_inbias = jnp.stack(
        [
            jnp.sum(query_low.astype(jnp.float32), axis=(0, 1)),
            jnp.sum(values_low.astype(jnp.float32), axis=(0, 1)),
        ]
    )
    terms = jnp.einsum("cblk,dck->bld", stacked, inproj, preferred_element_type=jnp.float32)
    summed = input_total(terms.reshape(-1, terms.shape[-1])).reshape(terms.shape)
    return (grad_inproj, grad_inbias, summed)


def time_project(normed, inproj, inbias, scale):
    linear = jnp.einsum("pfd,dck->cfkp", normed, inproj, preferred_element_type=jnp.float32)
    split = (linear.shape[1], linear.shape[2] // HEAD, HEAD, linear.shape[3])
    query = ((linear[0] + inbias[0][:, None]) * scale).astype(jnp.bfloat16).reshape(split)
    keys = linear[1].astype(jnp.bfloat16).reshape(split)
    values = (linear[2] + inbias[1][:, None]).astype(jnp.bfloat16).reshape(split)
    return (query, keys, values)


def time_forward(query, keys, values):
    scores = jnp.einsum("ihep,jhep->hijp", query, keys, preferred_element_type=jnp.float32)
    peak = jnp.max(scores, axis=2, keepdims=True)
    expon = jnp.exp(scores - peak)
    totals = jnp.sum(expon, axis=2, keepdims=True)
    logsum = peak + jnp.log(totals)
    probs = (expon / totals).astype(jnp.bfloat16)
    mixed = jnp.einsum("hijp,jhep->ihep", probs, values, preferred_element_type=jnp.float32)
    return (mixed.astype(jnp.bfloat16), logsum)


def time_backward(query, keys, values, logsum, d_mixed):
    scores = jnp.einsum("ihep,jhep->hijp", query, keys, preferred_element_type=jnp.float32)
    probs = jnp.exp(scores - logsum)
    d_values = jnp.einsum(
        "hijp,ihep->jhep", probs.astype(jnp.bfloat16), d_mixed, preferred_element_type=jnp.float32
    )
    d_probs = jnp.einsum("ihep,jhep->hijp", d_mixed, values, preferred_element_type=jnp.float32)
    inner = jnp.sum(probs * d_probs, axis=2, keepdims=True)
    d_scores = (probs * (d_probs - inner)).astype(jnp.bfloat16)
    d_query = jnp.einsum("hijp,jhep->ihep", d_scores, keys, preferred_element_type=jnp.float32)
    d_keys = jnp.einsum("hijp,ihep->jhep", d_scores, query, preferred_element_type=jnp.float32)
    return (d_query, d_keys, d_values)


def time_inproj_back(d_query, d_keys, d_values, normed, inproj, scale):
    flat = (d_query.shape[0], d_query.shape[1] * d_query.shape[2], d_query.shape[3])
    query_low = d_query.reshape(flat).astype(jnp.bfloat16) * scale
    keys_low = d_keys.reshape(flat).astype(jnp.bfloat16)
    values_low = d_values.reshape(flat).astype(jnp.bfloat16)
    stacked = jnp.stack([query_low, keys_low, values_low])
    grad_inproj = jnp.einsum("pfd,cfkp->dck", normed, stacked, preferred_element_type=jnp.float32)
    grad_inbias = jnp.stack(
        [
            jnp.sum(query_low.astype(jnp.float32), axis=(0, 2)),
            jnp.sum(values_low.astype(jnp.float32), axis=(0, 2)),
        ]
    )
    terms = jnp.einsum("cfkp,dck->pfd", stacked, inproj, preferred_element_type=jnp.float32)
    summed = input_total(terms.reshape(-1, terms.shape[-1])).reshape(terms.shape)
    return (grad_inproj, grad_inbias, summed)


def local(
    clips,
    cotangent,
    live,
    time_gain,
    time_shift,
    time_inproj,
    time_inbias,
    time_outproj,
    time_outbias,
    time_mixer,
    time_mixbias,
    space_gain,
    space_shift,
    space_inproj,
    space_inbias,
    space_outproj,
    space_outbias,
    feed_gain,
    feed_shift,
    feed_upward,
    feed_upbias,
    feed_down,
    feed_downbias,
):
    scale = HEAD ** (-0.5)
    width = clips.shape[2]
    half = width // lax.axis_size("tensor")
    tensor_rank = lax.axis_index("tensor")
    weight_live = live.astype(jnp.float32)[0]
    source = clips[0].astype(jnp.float32)
    class_row = source[0]
    grid_rows = source[1:].reshape(PLACES, FRAMES, width)
    time_normed = layer_norm(grid_rows, time_gain, time_shift).astype(jnp.bfloat16)
    t_query, t_keys, t_values = time_project(time_normed, time_inproj, time_inbias, scale)
    t_mixed, t_logsum = time_forward(t_query, t_keys, t_values)
    t_flat = jnp.transpose(t_mixed, (3, 0, 1, 2)).reshape(PLACES * FRAMES, half)
    proj_terms = jnp.dot(t_flat, time_outproj, preferred_element_type=jnp.float32)
    proj_half = lax.psum_scatter(proj_terms, "tensor", scatter_dimension=1, tiled=True)
    bias_half = lax.dynamic_slice_in_dim(time_outbias, tensor_rank * half, half)
    mixer_in = (proj_half + bias_half).astype(jnp.bfloat16)
    time_branch = (
        branch_total(jnp.dot(mixer_in, time_mixer, preferred_element_type=jnp.float32))
        + time_mixbias
    )
    after_time = grid_rows.reshape(PLACES * FRAMES, width) + time_branch
    frame_rows = jnp.transpose(after_time.reshape(PLACES, FRAMES, width), (1, 0, 2))
    space_in = jnp.concatenate(
        [jnp.broadcast_to(class_row, (FRAMES, 1, width)), frame_rows], axis=1
    )
    space_normed = layer_norm(space_in, space_gain, space_shift).astype(jnp.bfloat16)
    s_query, s_keys, s_values = project_heads(space_normed, space_inproj, space_inbias, scale)
    s_mixed, s_logsum = attend_forward(s_query, s_keys, s_values)
    s_flat = merge_heads(s_mixed).reshape(FRAMES * (PLACES + 1), half)
    space_terms = jnp.dot(s_flat, space_outproj, preferred_element_type=jnp.float32)
    space_branch = branch_total(space_terms).reshape(FRAMES, PLACES + 1, width) + space_outbias
    class_after = class_row + jnp.mean(space_branch[:, 0], axis=0)
    grid_after = after_time + jnp.transpose(space_branch[:, 1:], (1, 0, 2)).reshape(
        PLACES * FRAMES, width
    )
    mid_rows = jnp.concatenate([class_after[None], grid_after], axis=0)
    feed_normed = layer_norm(mid_rows, feed_gain, feed_shift).astype(jnp.bfloat16)
    hidden_pre = jnp.dot(feed_normed, feed_upward, preferred_element_type=jnp.float32) + feed_upbias
    hidden_act = jax.nn.gelu(hidden_pre, approximate=False).astype(jnp.bfloat16)
    feed_branch = (
        branch_total(jnp.dot(hidden_act, feed_down, preferred_element_type=jnp.float32))
        + feed_downbias
    )
    result = ((mid_rows + feed_branch) * weight_live).astype(jnp.bfloat16)
    grad_out = cotangent[0].astype(jnp.float32) * weight_live
    grad_low = grad_out.astype(jnp.bfloat16)
    g_feed_downbias = jnp.sum(grad_out, axis=0)
    g_feed_down = jnp.einsum("tf,td->fd", hidden_act, grad_low, preferred_element_type=jnp.float32)
    d_act = jnp.einsum("td,fd->tf", grad_low, feed_down, preferred_element_type=jnp.float32)
    _, gelu_pull = jax.vjp(lambda field: jax.nn.gelu(field, approximate=False), hidden_pre)
    d_pre = gelu_pull(d_act)[0].astype(jnp.bfloat16)
    g_feed_upbias = jnp.sum(d_pre.astype(jnp.float32), axis=0)
    g_feed_upward = jnp.einsum("td,tf->df", feed_normed, d_pre, preferred_element_type=jnp.float32)
    d_feed_normed = input_total(
        jnp.einsum("tf,df->td", d_pre, feed_upward, preferred_element_type=jnp.float32)
    )
    d_mid_ln, g_feed_gain, g_feed_shift = norm_back(mid_rows, feed_gain, feed_shift, d_feed_normed)
    d_mid = grad_out + d_mid_ln
    d_space = jnp.concatenate(
        [
            jnp.broadcast_to(d_mid[0] / FRAMES, (FRAMES, 1, width)),
            jnp.transpose(d_mid[1:].reshape(PLACES, FRAMES, width), (1, 0, 2)),
        ],
        axis=1,
    )
    g_space_outbias = jnp.sum(d_space, axis=(0, 1))
    d_space_low = d_space.reshape(FRAMES * (PLACES + 1), width).astype(jnp.bfloat16)
    g_space_outproj = jnp.einsum(
        "rk,rd->kd", s_flat, d_space_low, preferred_element_type=jnp.float32
    )
    d_s_mixed = jnp.einsum(
        "rd,kd->rk", d_space_low, space_outproj, preferred_element_type=jnp.float32
    )
    d_s_mixed = heads_of(d_s_mixed.astype(jnp.bfloat16).reshape(FRAMES, PLACES + 1, half))
    s_dquery, s_dkeys, s_dvalues = attend_backward(s_query, s_keys, s_values, s_logsum, d_s_mixed)
    g_space_inproj, g_space_inbias, d_space_normed = inproj_back(
        s_dquery, s_dkeys, s_dvalues, space_normed, space_inproj, scale
    )
    d_space_in, g_space_gain, g_space_shift = norm_back(
        space_in, space_gain, space_shift, d_space_normed
    )
    d_class = d_mid[0] + jnp.sum(d_space_in[:, 0], axis=0)
    d_grid = d_mid[1:] + jnp.transpose(d_space_in[:, 1:], (1, 0, 2)).reshape(PLACES * FRAMES, width)
    g_time_mixbias = jnp.sum(d_grid, axis=0)
    d_grid_low = d_grid.astype(jnp.bfloat16)
    g_time_mixer = jnp.einsum("rk,rd->kd", mixer_in, d_grid_low, preferred_element_type=jnp.float32)
    d_mixer_half = jnp.einsum(
        "rd,kd->rk", d_grid_low, time_mixer, preferred_element_type=jnp.float32
    ).astype(jnp.bfloat16)
    d_mixer_in = lax.all_gather(d_mixer_half, "tensor", axis=1, tiled=True)
    g_time_outbias = jnp.sum(d_mixer_in.astype(jnp.float32), axis=0)
    g_time_outproj = jnp.einsum("rk,rd->kd", t_flat, d_mixer_in, preferred_element_type=jnp.float32)
    d_t_mixed = jnp.einsum(
        "rd,kd->rk", d_mixer_in, time_outproj, preferred_element_type=jnp.float32
    )
    d_t_mixed = d_t_mixed.astype(jnp.bfloat16).reshape(PLACES, FRAMES, half // HEAD, HEAD)
    d_t_mixed = jnp.transpose(d_t_mixed, (1, 2, 3, 0))
    t_dquery, t_dkeys, t_dvalues = time_backward(t_query, t_keys, t_values, t_logsum, d_t_mixed)
    g_time_inproj, g_time_inbias, d_time_normed = time_inproj_back(
        t_dquery, t_dkeys, t_dvalues, time_normed, time_inproj, scale
    )
    d_grid_ln, g_time_gain, g_time_shift = norm_back(
        grid_rows, time_gain, time_shift, d_time_normed
    )
    d_source = jnp.concatenate(
        [d_class[None], d_grid + d_grid_ln.reshape(PLACES * FRAMES, width)], axis=0
    )
    settled = (
        lax.psum_scatter(g_time_gain, "dp", scatter_dimension=0, tiled=True),
        lax.psum_scatter(g_time_shift, "dp", scatter_dimension=0, tiled=True),
        lax.psum_scatter(g_time_inproj, "dp", scatter_dimension=0, tiled=True),
        lax.psum_scatter(g_time_inbias, "dp", scatter_dimension=1, tiled=True),
        lax.psum_scatter(g_time_outproj, "dp", scatter_dimension=1, tiled=True),
        lax.psum_scatter(g_time_outbias, "dp", scatter_dimension=0, tiled=True),
        lax.psum_scatter(g_time_mixer, "dp", scatter_dimension=1, tiled=True),
        lax.psum_scatter(g_time_mixbias, "dp", scatter_dimension=0, tiled=True),
        lax.psum_scatter(g_space_gain, "dp", scatter_dimension=0, tiled=True),
        lax.psum_scatter(g_space_shift, "dp", scatter_dimension=0, tiled=True),
        lax.psum_scatter(g_space_inproj, "dp", scatter_dimension=0, tiled=True),
        lax.psum_scatter(g_space_inbias, "dp", scatter_dimension=1, tiled=True),
        lax.psum_scatter(g_space_outproj, "dp", scatter_dimension=1, tiled=True),
        lax.psum_scatter(g_space_outbias, "dp", scatter_dimension=0, tiled=True),
        lax.psum_scatter(g_feed_gain, "dp", scatter_dimension=0, tiled=True),
        lax.psum_scatter(g_feed_shift, "dp", scatter_dimension=0, tiled=True),
        lax.psum_scatter(g_feed_upward, "dp", scatter_dimension=0, tiled=True),
        lax.psum_scatter(g_feed_upbias, "dp", scatter_dimension=0, tiled=True),
        lax.psum_scatter(g_feed_down, "dp", scatter_dimension=1, tiled=True),
        lax.psum_scatter(g_feed_downbias, "dp", scatter_dimension=0, tiled=True),
    )
    return (result[None], d_source.astype(jnp.bfloat16)[None]) + tuple(settled)


def solution(mesh):
    in_specs = (
        P("dp", None, None),
        P("dp", None, None),
        P("dp"),
        P(),
        P(),
        P(None, None, "tensor"),
        P(None, "tensor"),
        P("tensor", None),
        P(),
        P("tensor", None),
        P(),
        P(),
        P(),
        P(None, None, "tensor"),
        P(None, "tensor"),
        P("tensor", None),
        P(),
        P(),
        P(),
        P(None, "tensor"),
        P("tensor"),
        P("tensor", None),
        P(),
    )
    out_specs = (
        P("dp", None, None),
        P("dp", None, None),
        P("dp"),
        P("dp"),
        P("dp", None, "tensor"),
        P(None, ("tensor", "dp")),
        P("tensor", "dp"),
        P("dp"),
        P("tensor", "dp"),
        P("dp"),
        P("dp"),
        P("dp"),
        P("dp", None, "tensor"),
        P(None, ("tensor", "dp")),
        P("tensor", "dp"),
        P("dp"),
        P("dp"),
        P("dp"),
        P("dp", "tensor"),
        P(("tensor", "dp")),
        P("tensor", "dp"),
        P("dp"),
    )
    return jax.shard_map(local, mesh=mesh, in_specs=in_specs, out_specs=out_specs, check_vma=False)
```

profile of v0, /device:TPU:0, one launch (start us, length us, event | category | flops | bytes accessed | tf_op | source)
XLA Modules:
  0.0 1553.3 jit_solution(17192771606838227918)
XLA Ops:
  15.0 4.9 fusion.70
  34.2 4.2 copy.171
  41.2 4.2 copy.170
  45.4 6.0 fusion.83
  65.4 4.4 copy.173
  77.0 5.2 reshape.441
  82.2 5.0 fusion.84
  87.3 15.4 reduce-scatter.17.cloned.1.call-done
  102.8 5.3 fusion.51
  108.2 13.9 reduce-scatter.19.cloned.1.call-done
  123.1 16.4 %all-gather.8.cloned.1.call-done = f32[1568,768]{1,0:T(8,128)} async-done(((f32[1568,384]{1,0:T(8,128)}), f32[1568,768]{1,0:T(8,128)}) %all-gather.8.cloned.1.call-update) | async-done | bytes 4816912 | tf_op jit(solution)/shard_map/all_gather | solution.py:32
  139.5 4.5 fusion.41
  151.5 4.2 convolution_bitcast_fusion
  168.8 3.9 fusion.82
  181.6 4.1 reshape_reshape.6
  185.7 5.0 fusion.85
  190.8 14.4 reduce-scatter.21.cloned.1.call-done
  205.9 16.7 %all-gather.10.cloned.1.call-done = f32[1576,768]{1,0:T(8,128)} async-done(((f32[1576,384]{1,0:T(8,128)}), f32[1576,768]{1,0:T(8,128)}) %all-gather.10.cloned.1.call-update) | async-done | bytes 4841488 | tf_op jit(solution)/shard_map/all_gather | solution.py:32
  222.6 5.2 reshape.443
  232.0 4.5 bitcast_add_fusion.2
  238.7 27.1 %multiply_convert_fusion.1 = (bf16[1569,1536]{1,0:T(8,128)(2,1)}, f32[1569,1536]{1,0:T(8,128)}, f32[1569,1536]{1,0:T(8,128)}) fusion(f32[1536]{0:T(1024)S(1)} %copy-done.92, bf16[768,1536]{1,0:T(8,128)(2,1)S(1)} %copy-done, f32[768]{0:T(1024)S(1)} %copy-done.93, f32[768]{0:T(1024)S(1)} %copy-done.78, f32[1569]{0:T(1024)S(1)} %fusion.61, ...), kind=kOutput, calls=%fused_computation.10 | convolution fusion | flops 3868024320 | bytes 31303944 | tf_op jit(solution)/shard_map/dot_general | solution.py:204
  265.7 11.3 convert_reduce_fusion
  279.3 5.6 fusion.87
  286.6 8.6 fusion.86
  295.2 4.1 reduce-scatter.25.cloned.1.call-done
  299.4 16.7 %reduce-scatter.23.cloned.1.call-done = f32[1569,384]{1,0:T(8,128)} async-done(((f32[1569,768]{1,0:T(8,128)}), f32[1569,384]{1,0:T(8,128)}) %reduce-scatter.23.cloned.1.call-update) | async-done | bytes 2410000 | tf_op jit(solution)/shard_map/reduce_scatter | solution.py:31
  316.2 17.4 %all-gather.14.cloned.1.call-done = f32[1569,768]{1,0:T(8,128)} async-done(((f32[1569,384]{1,0:T(8,128)}), f32[1569,768]{1,0:T(8,128)}) %all-gather.14.cloned.1.call-update) | async-done | bytes 4819984 | tf_op jit(solution)/shard_map/all_gather | solution.py:37
  333.7 5.9 multiply_reduce_fusion.2
  339.6 11.5 all-gather.12.cloned.1.call-done
  351.1 7.6 fusion.78
  377.7 9.9 multiply_reduce_fusion
  387.7 11.2 multiply_convert_fusion
  398.9 5.4 convert_reduce_fusion.5
  404.3 5.3 convolution_convert_fusion.4
  419.9 8.3 convolution_bitcast_fusion.3
  428.2 5.2 reshape.446
  433.4 14.4 reduce-scatter.27.cloned.1.call-done
  448.2 5.2 concatenate.29
  453.4 11.9 all-gather.16.cloned.1.call-done
  465.3 4.8 multiply_reduce_fusion.4
  470.4 6.5 multiply_reduce_fusion.3
  477.0 5.2 reshape.447
  482.2 4.9 fusion.9
  499.7 9.4 all-gather.18.cloned.1.call-done
  515.5 6.2 fusion.35
  527.8 5.8 convert_reduce_fusion.3
  555.2 6.1 convolution_bitcast_fusion.2
  565.1 13.9 reduce-scatter.29.cloned.1.call-done
  579.1 11.2 fusion.74
  590.6 11.0 fusion.26
  601.7 4.3 fusion.89
  606.1 9.4 convolution_bitcast_fusion.4
  615.6 5.8 fusion.44
  621.7 4.3 fusion.88
  626.2 10.5 fusion.27
  645.9 5.2 multiply_reduce_fusion.7
  651.2 78.6 %all-reduce.13 = (f32[768]{0:T(1024)S(1)}, f32[768]{0:T(1024)S(1)}, f32[2,384]{1,0:T(2,128)S(1)}, f32[768]{0:T(1024)S(1)}, f32[768]{0:T(1024)S(1)}, /*index=5*/f...) all-reduce(f32[768]{0:T(1024)S(1)} %get-tuple-element.26, ...), channel_id=9, replica_groups=mesh['dp'=16,'tensor'=2] {'dp'}, use_global_device_ids=true, to_apply=%region_28.0.clone | all-reduce | flops 10752 | bytes 86016
  736.9 6.0 fusion.77
  745.6 136.1 %reduce-scatter.43.cloned.1.call-done = f32[1536,48]{0,1:T(8,128)} async-done(((f32[1536,768]{0,1:T(8,128)}), f32[1536,48]{0,1:T(8,128)}) %reduce-scatter.43.cloned.1.call-update) | async-done | bytes 294928 | tf_op jit(solution)/shard_map/reduce_scatter | solution.py:293
  881.7 128.7 %reduce-scatter.39.cloned.1.call-done = f32[384,48]{0,1:T(8,128)} async-done(((f32[384,768]{0,1:T(8,128)}), f32[384,48]{0,1:T(8,128)}) %reduce-scatter.39.cloned.1.call-update) | async-done | bytes 73744 | tf_op jit(solution)/shard_map/reduce_scatter | solution.py:287
  1010.4 139.0 %reduce-scatter.37.cloned.1.call-done = f32[48,3,384]{2,0,1:T(8,128)} async-done(((f32[768,3,384]{2,0,1:T(8,128)}), f32[48,3,384]{2,0,1:T(8,128)}) %reduce-scatter.37.cloned.1.call-update) | async-done | bytes 221200 | tf_op jit(solution)/shard_map/reduce_scatter | solution.py:285
  1149.4 128.8 %reduce-scatter.35.cloned.1.call-done = f32[384,48]{0,1:T(8,128)} async-done(((f32[384,768]{0,1:T(8,128)}), f32[384,48]{0,1:T(8,128)}) %reduce-scatter.35.cloned.1.call-update) | async-done | bytes 73744 | tf_op jit(solution)/shard_map/reduce_scatter | solution.py:281
  1278.3 128.5 %reduce-scatter.33.cloned.1.call-done = f32[384,48]{0,1:T(8,128)} async-done(((f32[384,768]{0,1:T(8,128)}), f32[384,48]{0,1:T(8,128)}) %reduce-scatter.33.cloned.1.call-update) | async-done | bytes 73744 | tf_op jit(solution)/shard_map/reduce_scatter | solution.py:279
  1406.8 139.2 %reduce-scatter.31.cloned.1.call-done = f32[48,3,384]{2,0,1:T(8,128)} async-done(((f32[768,3,384]{2,0,1:T(8,128)}), f32[48,3,384]{2,0,1:T(8,128)}) %reduce-scatter.31.cloned.1.call-update) | async-done | bytes 221200 | tf_op jit(solution)/shard_map/reduce_scatter | solution.py:277
  (391 shorter events, 184.8 us)
Async XLA Ops:
  7.2 231.4 %copy-start = (bf16[768,1536]{1,0:T(8,128)(2,1)S(1)}, bf16[768,1536]{1,0:T(8,128)(2,1)}, u32[]{:S(2)}) copy-start(bf16[768,1536]{1,0:T(8,128)(2,1)} %param.42) | copy-start | bytes 7077892
  7.2 95.6 %reduce-scatter.17.cloned.1.call-start = ((), (), s32[]{:S(2)}) async-start(), calls=%async_computation.14 | async-start | bytes 7225344 | tf_op jit(solution)/shard_map/reduce_scatter | solution.py:180
  14.8 8.6 copy-start.44
  14.9 8.4 copy-start.60
  15.0 8.3 copy-start.62
  54.8 7.1 copy-start.23
  73.6 8.6 copy-start.32
  82.2 20.6 %copy-start.25 = (bf16[384,768]{1,0:T(8,128)(2,1)S(1)}, bf16[384,768]{1,0:T(8,128)(2,1)}, u32[]{:S(2)}) copy-start(bf16[384,768]{1,0:T(8,128)(2,1)} %param.32) | copy-start | bytes 1769476
  87.2 34.9 %reduce-scatter.19.cloned.1.call-start = ((), (), s32[]{:S(2)}) async-start(), calls=%async_computation.15 | async-start | bytes 7225344 | tf_op jit(solution)/shard_map/reduce_scatter | solution.py:31
  87.3 20.7 %copy-start.64 = (f32[384]{0:T(512)}, f32[384]{0:T(512)S(1)}, u32[]{:S(2)}) copy-start(f32[384]{0:T(512)S(1)} %dynamic_slice.3) | copy-start | bytes 4612
  108.1 14.1 copy-start.86
  108.1 31.4 %copy-start.79 = (f32[768]{0:T(1024)S(1)}, f32[768]{0:T(1024)}, u32[]{:S(2)}) copy-start(f32[768]{0:T(1024)} %param.33) | copy-start | bytes 9220
  108.1 31.4 %all-gather.8.cloned.1.call-start = ((), (), s32[]{:S(2)}) async-start(), calls=%async_computation.16 | async-start | bytes 7225344 | tf_op jit(solution)/shard_map/all_gather | solution.py:32
  122.1 83.1 %reduce-scatter.21.cloned.1.call-start = ((), (), s32[]{:S(2)}) async-start(), calls=%async_computation.17 | async-start | bytes 7262208 | tf_op jit(solution)/shard_map/reduce_scatter | solution.py:31
  122.3 46.6 %copy-start.56 = (f32[6,64]{1,0:T(8,128)}, f32[6,64]{1,0:T(8,128)S(1)}, u32[]{:S(2)}) copy-start(f32[6,64]{1,0:T(8,128)S(1)} %add.270) | copy-start | bytes 4612
  122.3 52.4 %copy-start.74 = (f32[6,64]{1,0:T(8,128)}, f32[6,64]{1,0:T(8,128)S(1)}, u32[]{:S(2)}) copy-start(f32[6,64]{1,0:T(8,128)S(1)} %add.267) | copy-start | bytes 4612
  179.5 6.2 copy-start.30
  190.7 31.8 %all-gather.10.cloned.1.call-start = ((), (), s32[]{:S(2)}) async-start(), calls=%async_computation.18 | async-start | bytes 7262208 | tf_op jit(solution)/shard_map/all_gather | solution.py:32
  205.2 94.2 %reduce-scatter.25.cloned.1.call-start = ((), (), s32[]{:S(2)}) async-start(), calls=%async_computation.21 | async-start | bytes 7262208 | tf_op jit(solution)/shard_map/reduce_scatter | solution.py:36
  205.9 21.9 %copy-start.81 = (f32[768]{0:T(1024)S(1)}, f32[768]{0:T(1024)}, u32[]{:S(2)}) copy-start(f32[768]{0:T(1024)} %param.39) | copy-start | bytes 9220
  238.6 27.1 %copy-start.17 = (bf16[1,1569,768]{2,1,0:T(8,128)(2,1)S(1)}, bf16[1,1569,768]{2,1,0:T(8,128)(2,1)}, u32[]{:S(2)}) copy-start(bf16[1,1569,768]{2,1,0:T(8,128)(2,1)} %param.24) | copy-start | bytes 7229956
  238.7 27.1 %copy-start.88 = (bf16[1536,768]{1,0:T(8,128)(2,1)S(1)}, bf16[1536,768]{1,0:T(8,128)(2,1)}, u32[]{:S(2)}) copy-start(bf16[1536,768]{1,0:T(8,128)(2,1)} %param.44) | copy-start | bytes 7077892
  284.9 31.2 %reduce-scatter.23.cloned.1.call-start = ((), (), s32[]{:S(2)}) async-start(), calls=%async_computation.19 | async-start | bytes 7262208 | tf_op jit(solution)/shard_map/reduce_scatter | solution.py:31
  295.2 21.0 %copy-start.29 = (f32[8,6,197]{2,1,0:T(8,128)S(1)}, f32[8,6,197]{2,1,0:T(8,128)}, u32[]{:S(2)}) copy-start(f32[8,6,197]{2,1,0:T(8,128)} %copy-done.28) | copy-start | bytes 113476
  295.2 21.0 %copy-start.37 = (f32[8,6,197]{2,1,0:T(8,128)S(1)}, f32[8,6,197]{2,1,0:T(8,128)}, u32[]{:S(2)}) copy-start(f32[8,6,197]{2,1,0:T(8,128)} %copy-done.36) | copy-start | bytes 113476
  295.2 38.5 %all-gather.14.cloned.1.call-start = ((), (), s32[]{:S(2)}) async-start(), calls=%async_computation.22 | async-start | bytes 7262208 | tf_op jit(solution)/shard_map/all_gather | solution.py:37
  299.4 51.7 %all-gather.12.cloned.1.call-start = ((), (), s32[]{:S(2)}) async-start(), calls=%async_computation.20 | async-start | bytes 7262208 | tf_op jit(solution)/shard_map/all_gather | solution.py:32
  316.1 131.7 %reduce-scatter.27.cloned.1.call-start = ((), (), s32[]{:S(2)}) async-start(), calls=%async_computation.23 | async-start | bytes 7262208 | tf_op jit(solution)/shard_map/reduce_scatter | solution.py:36
  316.2 34.9 %copy-start.84 = (f32[768]{0:T(1024)S(1)}, f32[768]{0:T(1024)}, u32[]{:S(2)}) copy-start(f32[768]{0:T(1024)} %param.45) | copy-start | bytes 9220
  351.1 7.6 copy-start.18
  370.8 6.9 copy-start.75
  377.7 9.9 copy-start.14
  387.6 11.2 copy-start.9
  398.9 10.7 slice-start
  398.9 10.7 slice-start.1
  433.4 14.8 copy-start.43
  433.4 31.9 %all-gather.16.cloned.1.call-start = ((), (), s32[]{:S(2)}) async-start(), calls=%async_computation.24 | async-start | bytes 7262208 | tf_op jit(solution)/shard_map/all_gather | solution.py:37
  447.9 61.3 %all-gather.18.cloned.1.call-start = ((), (), s32[]{:S(2)}) async-start(), calls=%async_computation.25 | async-start | bytes 3612672 | tf_op jit(solution)/shard_map/all_gather | solution.py:256
  448.2 17.1 %copy-start.51 = (f32[768]{0:T(1024)S(1)}, f32[768]{0:T(1024)}, u32[]{:S(2)}) copy-start(f32[768]{0:T(1024)} %param.34) | copy-start | bytes 9220
  453.4 16.8 %copy-start.49 = (f32[8,197]{1,0:T(8,128)S(1)}, f32[8,197]{1,0:T(8,128)}, u32[]{:S(2)}) copy-start(f32[8,197]{1,0:T(8,128)} %copy-done.48) | copy-start | bytes 18916
  477.0 12.7 slice-start.7
  482.2 7.5 slice-start.8
  494.3 14.8 copy-start.33
  496.9 82.1 %reduce-scatter.29.cloned.1.call-start = ((), (), s32[]{:S(2)}) async-start(), calls=%async_computation.26 | async-start | bytes 7225344 | tf_op jit(solution)/shard_map/reduce_scatter | solution.py:36
  565.0 14.1 copy-start.94
  565.0 80.8 %all-gather.20.cloned.1.call-start = ((), (), s32[]{:S(2)}) async-start(), calls=%async_computation.27 | async-start | bytes 7225344 | tf_op jit(solution)/shard_map/all_gather | solution.py:37
  579.0 166.6 %reduce-scatter.41.cloned.1.call-start = ((), (), s32[]{:S(2)}) async-start(), calls=%async_computation.33 | async-start | bytes 5013504 | tf_op jit(solution)/shard_map/reduce_scatter | solution.py:291
  590.3 11.4 copy-start.21
  590.3 291.4 %reduce-scatter.43.cloned.1.call-start = ((), (), s32[]{:S(2)}) async-start(), calls=%async_computation.34 | async-start | bytes 5013504 | tf_op jit(solution)/shard_map/reduce_scatter | solution.py:293
  601.7 408.8 %reduce-scatter.39.cloned.1.call-start = ((), (), s32[]{:S(2)}) async-start(), calls=%async_computation.32 | async-start | bytes 1253376 | tf_op jit(solution)/shard_map/reduce_scatter | solution.py:287
  606.0 9.5 copy-start.65
  606.0 543.4 %reduce-scatter.37.cloned.1.call-start = ((), (), s32[]{:S(2)}) async-start(), calls=%async_computation.31 | async-start | bytes 3760128 | tf_op jit(solution)/shard_map/reduce_scatter | solution.py:285
  615.5 6.2 copy-start.20
  615.5 662.7 %reduce-scatter.35.cloned.1.call-start = ((), (), s32[]{:S(2)}) async-start(), calls=%async_computation.30 | async-start | bytes 1253376 | tf_op jit(solution)/shard_map/reduce_scatter | solution.py:281
  621.4 785.3 %reduce-scatter.33.cloned.1.call-start = ((), (), s32[]{:S(2)}) async-start(), calls=%async_computation.29 | async-start | bytes 1253376 | tf_op jit(solution)/shard_map/reduce_scatter | solution.py:279
  626.1 10.7 copy-start.97
  626.1 919.8 %reduce-scatter.31.cloned.1.call-start = ((), (), s32[]{:S(2)}) async-start(), calls=%async_computation.28 | async-start | bytes 3760128 | tf_op jit(solution)/shard_map/reduce_scatter | solution.py:277
  636.7 6.8 copy-start.76
  636.7 6.8 copy-start.77
  636.7 9.1 copy-start.39
  636.7 9.1 copy-start.45
  645.8 91.1 %copy-start.47 = (f32[1568]{0:T(1024)S(1)}, f32[1568]{0:T(1024)}, u32[]{:S(2)}) copy-start(f32[1568]{0:T(1024)} %copy-done.46) | copy-start | bytes 18820
  645.9 97.0 %slice-start.5 = ((s8[4816896]{0:T(1024)(128)(4,1)}), s8[622592]{0:T(1024)(128)(4,1)S(1)}, s32[]{:S(2)}) async-start(s8[4816896]{0:T(1024)(128)(4,1)} %bitcast.216), calls=%async_computation.40 | async-start | bytes 1245184
  742.9 803.0 %copy-start.1 = (bf16[768,1536]{1,0:T(8,128)(2,1)S(1)}, bf16[768,1536]{1,0:T(8,128)(2,1)}, u32[]{:S(2)}) copy-start(bf16[768,1536]{1,0:T(8,128)(2,1)} %param.42) | copy-start | bytes 7077892
  (65 other events, 250.2 us)
Sparse Core Ops, SparseCore 0:
  87.3 15.3 reduce-scatter.16
  108.2 13.7 reduce-scatter.18
  123.6 15.8 all-gather.7
  190.8 14.2 reduce-scatter.20
  206.6 15.8 all-gather.9
  285.0 14.2 reduce-scatter.24
  301.7 14.3 reduce-scatter.22
  317.7 15.9 all-gather.13
  335.3 15.7 all-gather.11
  433.5 14.2 reduce-scatter.26
  449.4 15.8 all-gather.15
  497.0 12.1 all-gather.17
  565.2 13.7 reduce-scatter.28
  580.5 15.8 all-gather.19
  602.7 137.8 reduce-scatter.40
  746.3 135.4 reduce-scatter.42
  887.6 122.7 reduce-scatter.38
  1016.8 132.6 reduce-scatter.36
  1155.5 122.7 reduce-scatter.34
  1284.1 122.5 reduce-scatter.32
  1413.2 132.6 reduce-scatter.30
where the time goes:
time: 1560 us; the launch traced here: 1550 us
  waiting for transfers between devices  977 us (63%)
  matrix products  214 us (14%)
  local copies, waits for them, and re-layouts  158 us (10%)
  other arithmetic  106 us (7%)
  blocking collectives  78.6 us (5%)
  between operations  18.8 us (1%)
    reduce_scatter x1, waiting for transfers between devices, local(): lax.psum_scatter(g_time_inproj, 'dp', scatter_dimension=0, tiled=True)  139 us
    reduce_scatter x1, waiting for transfers between devices, local(): lax.psum_scatter(g_space_inproj, 'dp', scatter_dimension=0, tiled=True)  139 us
    reduce_scatter x1, waiting for transfers between devices, local(): lax.psum_scatter(g_feed_down, 'dp', scatter_dimension=1, tiled=True)  136 us
    reduce_scatter x1, waiting for transfers between devices, local(): lax.psum_scatter(g_time_mixer, 'dp', scatter_dimension=1, tiled=True)  129 us
    reduce_scatter x1, waiting for transfers between devices, local(): lax.psum_scatter(g_space_outproj, 'dp', scatter_dimension=1, tiled=True)  129 us
    reduce_scatter x1, waiting for transfers between devices, local(): lax.psum_scatter(g_time_outproj, 'dp', scatter_dimension=1, tiled=True)  128 us
    unnamed x1, blocking collectives  78.6 us
    reduce_scatter x3, waiting for transfers between devices, branch_total(): lax.psum_scatter(terms, 'tensor', scatter_dimension=1, tiled=True)  45 us
  transfers between devices with their start and end apart: 21, of which 19 were waited for; matrix products, arithmetic and copies ran while one was open for 7% of the time, Pallas kernels for 0%

commit v1 on v0

--- a/solution.py
+++ b/solution.py
@@ -27,14 +27,72 @@
     return field.reshape(field.shape[:-2] + (field.shape[-2] * field.shape[-1],))
 
 
+def swap_tensor(field):
+    size = lax.axis_size("tensor")
+    return lax.ppermute(field, "tensor", [(i, i ^ 1) for i in range(size)])
+
+
 def branch_total(terms):
-    half_sum = lax.psum_scatter(terms, "tensor", scatter_dimension=1, tiled=True)
-    return lax.all_gather(half_sum, "tensor", axis=1, tiled=True)
+    low = terms.astype(jnp.bfloat16)
+    other = swap_tensor(low)
+    return low.astype(jnp.float32) + other.astype(jnp.float32)
+
+
+def add_low(left, right):
+    return (left.astype(jnp.float32) + right.astype(jnp.float32)).astype(jnp.bfloat16)
+
+
+def halve(field, axis, bit, size, keep_bit):
+    keep = lax.dynamic_index_in_dim(field, keep_bit, axis, keepdims=False)
+    send = lax.dynamic_index_in_dim(field, 1 - keep_bit, axis, keepdims=False)
+    got = lax.ppermute(send, "dp", [(i, i ^ bit) for i in range(size)])
+    return add_low(keep, got)
+
+
+def line_total(field, stride, size):
+    count = field.shape[0]
+    place = (lax.axis_index("dp") // stride) % count
+    def at(offset):
+        return lax.dynamic_index_in_dim(field, jnp.clip(place + offset, 0, count - 1), 0, keepdims=False)
+    up = at(count - 1)
+    down = at(1 - count)
+    for step in range(1, count):
+        ups = [(i, i + stride) for i in range(size) if (i // stride) % count < step and (i // stride) % count + 1 < count]
+        downs = [(i, i - stride) for i in range(size) if (i // stride) % count > count - 1 - step]
+        got_up = lax.ppermute(up, "dp", ups)
+        got_down = lax.ppermute(down, "dp", downs)
+        if step < count - 1:
+            up = add_low(at(count - 1 - step), got_up)
+            down = add_low(at(step + 1 - count), got_down)
+    return (at(0).astype(jnp.float32) + got_up.astype(jnp.float32)) + got_down.astype(jnp.float32)
+
+
+def dp_totals(first, second):
+    size = lax.axis_size("dp")
+    me = lax.axis_index("dp")
+    if size == 16:
+        def split(field):
+            return field.reshape((4, 2, 2) + field.shape[1:])
+        x_bit = me % 2
+        y_bit = (me // 2) % 2
+        first = halve(split(first), 2, 1, size, x_bit)
+        second = halve(split(second), 1, 2, size, y_bit)
+        first = halve(first, 1, 2, size, y_bit)
+        second = halve(second, 1, 1, size, x_bit)
+        return line_total(first, 4, size), line_total(second, 4, size)
+    out = []
+    for field in (first, second):
+        span = size // 2
+        while span >= 1:
+            field = field.reshape((2, span) + field.shape[1:])
+            field = halve(field, 0, span, size, (me // span) % 2)
+            span //= 2
+        out.append(field[0].astype(jnp.float32))
+    return tuple(out)
 
 
 def input_total(terms):
-    half_sum = lax.psum_scatter(terms, "tensor", scatter_dimension=1, tiled=True)
-    return lax.all_gather(half_sum, "tensor", axis=1, tiled=True)
+    return branch_total(terms)
 
 
 def project_heads(normed, inproj, inbias, scale):
@@ -177,7 +235,10 @@
     t_mixed, t_logsum = time_forward(t_query, t_keys, t_values)
     t_flat = jnp.transpose(t_mixed, (3, 0, 1, 2)).reshape(PLACES * FRAMES, half)
     proj_terms = jnp.dot(t_flat, time_outproj, preferred_element_type=jnp.float32)
-    proj_half = lax.psum_scatter(proj_terms, "tensor", scatter_dimension=1, tiled=True)
+    proj_low = proj_terms.astype(jnp.bfloat16)
+    kept = lax.dynamic_slice_in_dim(proj_low, tensor_rank * half, half, 1)
+    sent = lax.dynamic_slice_in_dim(proj_low, (1 - tensor_rank) * half, half, 1)
+    proj_half = kept.astype(jnp.float32) + swap_tensor(sent).astype(jnp.float32)
     bias_half = lax.dynamic_slice_in_dim(time_outbias, tensor_rank * half, half)
     mixer_in = (proj_half + bias_half).astype(jnp.bfloat16)
     time_branch = (
@@ -211,7 +272,7 @@
     grad_out = cotangent[0].astype(jnp.float32) * weight_live
     grad_low = grad_out.astype(jnp.bfloat16)
     g_feed_downbias = jnp.sum(grad_out, axis=0)
-    g_feed_down = jnp.einsum("tf,td->fd", hidden_act, grad_low, preferred_element_type=jnp.float32)
+    g_feed_down = jnp.einsum("tf,td->df", hidden_act, grad_low, preferred_element_type=jnp.float32)
     d_act = jnp.einsum("td,fd->tf", grad_low, feed_down, preferred_element_type=jnp.float32)
     _, gelu_pull = jax.vjp(lambda field: jax.nn.gelu(field, approximate=False), hidden_pre)
     d_pre = gelu_pull(d_act)[0].astype(jnp.bfloat16)
@@ -232,7 +293,7 @@
     g_space_outbias = jnp.sum(d_space, axis=(0, 1))
     d_space_low = d_space.reshape(FRAMES * (PLACES + 1), width).astype(jnp.bfloat16)
     g_space_outproj = jnp.einsum(
-        "rk,rd->kd", s_flat, d_space_low, preferred_element_type=jnp.float32
+        "rk,rd->dk", s_flat, d_space_low, preferred_element_type=jnp.float32
     )
     d_s_mixed = jnp.einsum(
         "rd,kd->rk", d_space_low, space_outproj, preferred_element_type=jnp.float32
@@ -249,13 +310,18 @@
     d_grid = d_mid[1:] + jnp.transpose(d_space_in[:, 1:], (1, 0, 2)).reshape(PLACES * FRAMES, width)
     g_time_mixbias = jnp.sum(d_grid, axis=0)
     d_grid_low = d_grid.astype(jnp.bfloat16)
-    g_time_mixer = jnp.einsum("rk,rd->kd", mixer_in, d_grid_low, preferred_element_type=jnp.float32)
+    g_time_mixer = jnp.einsum("rk,rd->dk", mixer_in, d_grid_low, preferred_element_type=jnp.float32)
     d_mixer_half = jnp.einsum(
         "rd,kd->rk", d_grid_low, time_mixer, preferred_element_type=jnp.float32
     ).astype(jnp.bfloat16)
-    d_mixer_in = lax.all_gather(d_mixer_half, "tensor", axis=1, tiled=True)
+    d_mixer_peer = swap_tensor(d_mixer_half)
+    d_mixer_in = jnp.where(
+        tensor_rank == 0,
+        jnp.concatenate([d_mixer_half, d_mixer_peer], axis=1),
+        jnp.concatenate([d_mixer_peer, d_mixer_half], axis=1),
+    )
     g_time_outbias = jnp.sum(d_mixer_in.astype(jnp.float32), axis=0)
-    g_time_outproj = jnp.einsum("rk,rd->kd", t_flat, d_mixer_in, preferred_element_type=jnp.float32)
+    g_time_outproj = jnp.einsum("rk,rd->dk", t_flat, d_mixer_in, preferred_element_type=jnp.float32)
     d_t_mixed = jnp.einsum(
         "rd,kd->rk", d_mixer_in, time_outproj, preferred_element_type=jnp.float32
     )
@@ -271,29 +337,56 @@
     d_source = jnp.concatenate(
         [d_class[None], d_grid + d_grid_ln.reshape(PLACES * FRAMES, width)], axis=0
     )
+    low = lambda field: field.astype(jnp.bfloat16)
+    dests = lax.axis_size("dp")
+    by_dest = lambda field: low(field).reshape(dests, width // dests, -1)
+    feed_up_sum, feed_down_sum = dp_totals(by_dest(g_feed_upward), by_dest(g_feed_down))
+    space_first = low(g_space_inproj[:, :2]).reshape(width, 2 * half)
+    space_second = jnp.concatenate([low(g_space_inproj[:, 2]), low(g_space_outproj)], axis=1)
+    space_a, space_b = dp_totals(by_dest(space_first), by_dest(space_second))
+    vectors = [
+        g_time_gain, g_time_shift, g_time_outbias, g_time_mixbias, g_space_gain, g_space_shift,
+        g_space_outbias, g_feed_gain, g_feed_shift, g_feed_downbias, g_time_inbias[0], g_time_inbias[1],
+        g_space_inbias[0], g_space_inbias[1], g_feed_upbias,
+    ]
+    packed = jnp.concatenate([low(v).reshape(dests, -1) for v in vectors], axis=1)
+    share = packed.shape[1]
+    rows = width // dests
+    packed = jnp.pad(packed, ((0, 0), (0, -share % (2 * half)))).reshape(dests, -1, 2 * half)
+    time_first = by_dest(g_time_inproj.reshape(width, 3 * half))
+    time_second = jnp.concatenate([low(g_time_outproj), low(g_time_mixer)], axis=1).reshape(dests, rows, -1)
+    time_second = jnp.concatenate([time_second, packed], axis=1)
+    time_a, time_b = dp_totals(time_first, time_second)
+    flat = time_b[rows:].reshape(-1)
+    pieces = []
+    at = 0
+    for v in vectors:
+        count = v.shape[0] // dests
+        pieces.append(flat[at : at + count])
+        at += count
     settled = (
-        lax.psum_scatter(g_time_gain, "dp", scatter_dimension=0, tiled=True),
-        lax.psum_scatter(g_time_shift, "dp", scatter_dimension=0, tiled=True),
-        lax.psum_scatter(g_time_inproj, "dp", scatter_dimension=0, tiled=True),
-        lax.psum_scatter(g_time_inbias, "dp", scatter_dimension=1, tiled=True),
-        lax.psum_scatter(g_time_outproj, "dp", scatter_dimension=1, tiled=True),
-        lax.psum_scatter(g_time_outbias, "dp", scatter_dimension=0, tiled=True),
-        lax.psum_scatter(g_time_mixer, "dp", scatter_dimension=1, tiled=True),
-        lax.psum_scatter(g_time_mixbias, "dp", scatter_dimension=0, tiled=True),
-        lax.psum_scatter(g_space_gain, "dp", scatter_dimension=0, tiled=True),
-        lax.psum_scatter(g_space_shift, "dp", scatter_dimension=0, tiled=True),
-        lax.psum_scatter(g_space_inproj, "dp", scatter_dimension=0, tiled=True),
-        lax.psum_scatter(g_space_inbias, "dp", scatter_dimension=1, tiled=True),
-        lax.psum_scatter(g_space_outproj, "dp", scatter_dimension=1, tiled=True),
-        lax.psum_scatter(g_space_outbias, "dp", scatter_dimension=0, tiled=True),
-        lax.psum_scatter(g_feed_gain, "dp", scatter_dimension=0, tiled=True),
-        lax.psum_scatter(g_feed_shift, "dp", scatter_dimension=0, tiled=True),
-        lax.psum_scatter(g_feed_upward, "dp", scatter_dimension=0, tiled=True),
-        lax.psum_scatter(g_feed_upbias, "dp", scatter_dimension=0, tiled=True),
-        lax.psum_scatter(g_feed_down, "dp", scatter_dimension=1, tiled=True),
-        lax.psum_scatter(g_feed_downbias, "dp", scatter_dimension=0, tiled=True),
-    )
-    return (result[None], d_source.astype(jnp.bfloat16)[None]) + tuple(settled)
+        pieces[0],
+        pieces[1],
+        time_a.reshape(rows, 3, half),
+        jnp.stack([pieces[10], pieces[11]]),
+        time_b[:rows, :half].T,
+        pieces[2],
+        time_b[:rows, half:].T,
+        pieces[3],
+        pieces[4],
+        pieces[5],
+        jnp.concatenate([space_a, space_b[:, :half]], axis=1).reshape(rows, 3, half),
+        jnp.stack([pieces[12], pieces[13]]),
+        space_b[:, half:].T,
+        pieces[6],
+        pieces[7],
+        pieces[8],
+        feed_up_sum,
+        pieces[14],
+        feed_down_sum.T,
+        pieces[9],
+    )
+    return (result[None], d_source.astype(jnp.bfloat16)[None]) + settled
 
 
 def solution(mesh):

time: 1560 us -> 713 us (0.46)
  waiting for transfers between devices: 977 us -> 97.9 us
  starting transfers between devices: 1.93 us -> 98 us
  blocking collectives: 78.6 us -> 0 us
  local copies, waits for them, and re-layouts: 158 us -> 184 us
  matrix products: 214 us -> 192 us
  other arithmetic: 106 us -> 124 us
    reduce_scatter x14 -> x0, waiting for transfers between devices: 893 us -> none  [the longest x1 139 us: local(): lax.psum_scatter(g_time_inproj, 'dp', scatter_dimension=0, tiled=True)]
    ppermute x0 -> x56, starting transfers between devices: none -> 98 us  [the longest x18 64.4 us: line_total(): got_up = lax.ppermute(up, 'dp', ups)]
    ppermute x0 -> x56, waiting for transfers between devices: none -> 97.9 us  [the longest x12 69.2 us: halve(): got = lax.ppermute(send, 'dp', [(i, i ^ bit) for i in range(size)])]
    all_gather x7 -> x0, waiting for transfers between devices: 83.3 us -> none  [the longest x3 44.6 us: branch_total(): return lax.all_gather(half_sum, 'tensor', axis=1, tiled=True)]
    unnamed x1 -> x0, blocking collectives: 78.6 us -> none
  transfers between devices with their start and end apart: 21 -> 56, of which waited for: 19 -> 19; matrix products, arithmetic and copies ran while one was open for 7% -> 17% of each run, Pallas kernels for 0% -> 0%
where the time goes in v1:
time: 713 us; the launch traced here: 700 us
  matrix products  192 us (27%)
  local copies, waits for them, and re-layouts  184 us (26%)
  other arithmetic  124 us (17%)
  starting transfers between devices  98 us (14%)
  waiting for transfers between devices  97.9 us (14%)
    ppermute x12, waiting for transfers between devices, halve(): got = lax.ppermute(send, 'dp', [(i, i ^ bit) for i in range(size)])  69.2 us
    ppermute x18, starting transfers between devices, line_total(): got_up = lax.ppermute(up, 'dp', ups)  64.4 us
    dot_general x1, matrix products, local(): jnp.dot(feed_normed, feed_upward, preferred_element_type=jnp.float32)  26.6 us
    reduce_sum x4, other arithmetic, layer_norm(): return center * lax.rsqrt(spread_sq + 1e-06) * gain + shift  23.1 us
    ppermute x18, starting transfers between devices, line_total(): got_down = lax.ppermute(down, 'dp', downs)  16.6 us
    ppermute x12, starting transfers between devices, halve(): got = lax.ppermute(send, 'dp', [(i, i ^ bit) for i in range(size)])  14.8 us
    dot_general x1, matrix products, local(): jnp.einsum('td,fd->tf', grad_low, feed_down, preferred_element_type=jnp.f...  14.6 us
    ppermute x18, waiting for transfers between devices, line_total(): got_down = lax.ppermute(down, 'dp', downs)  14.6 us
  transfers between devices with their start and end apart: 56, of which 19 were waited for; matrix products, arithmetic and copies ran while one was open for 17% of the time, Pallas kernels for 0%

profile of v1, /device:TPU:0, one launch (start us, length us, event | category | flops | bytes accessed | tf_op | source)
XLA Modules:
  0.0 700.3 jit_solution(7268719134267813495)
XLA Ops:
  8.6 4.7 fusion.115
  27.5 4.2 copy.276
  34.6 4.2 copy.275
  38.8 6.0 fusion.135
  58.5 4.6 copy.278
  70.2 5.2 reshape.607
  75.4 4.5 convolution_convert_fusion.6
  85.6 4.5 convolution_convert_fusion.5
  95.0 4.9 fusion.46
  106.1 4.2 convolution_bitcast_fusion.1
  136.1 4.2 reshape_reshape.18
  140.2 4.2 convolution_convert_fusion.4
  151.5 5.1 concatenate.55
  157.3 5.0 convert_add_fusion.2
  162.3 5.1 reshape.609
  171.6 4.4 bitcast_add_fusion.2
  178.4 26.6 %multiply_convert_fusion.1 = (bf16[1569,1536]{1,0:T(8,128)(2,1)S(1)}, f32[1569,1536]{1,0:T(8,128)}, f32[1569,1536]{1,0:T(8,128)}) fusion(f32[1536]{0:T(1024)S(1)} %copy-done.98, bf16[768,1536]{1,0:T(8,128)(2,1)S(1)} %copy-done, f32[768]{0:T(1024)S(1)} %copy-done.99, f32[768]{0:T(1024)S(1)} %copy-done.76, f32[1569]{0:T(1024)S(1)} %fusion.107, ...), kind=kOutput, calls=%fused_computation.9 | convolution fusion | flops 3868024320 | bytes 31303944 | tf_op jit(solution)/shard_map/dot_general | solution.py:265
  205.0 14.6 %fusion.134 = (bf16[1536]{0:T(1024)(128)(2,1)}, bf16[1569,1536]{1,0:T(8,128)(2,1)}) fusion(f32[1569,1536]{1,0:T(8,128)} %get-tuple-element.133, f32[1569,1536]{1,0:T(8,128)} %get-tuple-element.203, bf16[1536,768]{1,0:T(8,128)(2,1)S(1)} %copy-done.91, bf16[1,1569,768]{2,1,0:T(8,128)(2,1)S(1)} %copy-done.18, f32[]{:T(128)} %bitcast.23), kind=kOutput, calls=%fused_computation.358 | convolution fusion | flops 3741498624 | bytes 28872196 | tf_op jit(solution)/shard_map/td,fd->tf/dot_general | solution.py:276
  219.6 7.8 %convolution_convert_fusion.1 = bf16[768,1536]{1,0:T(8,128)(2,1)S(1)} fusion(bf16[1569,1536]{1,0:T(8,128)(2,1)} %get-tuple-element.215, f32[768]{0:T(1024)S(1)} %copy-done.99, f32[768]{0:T(1024)S(1)} %copy-done.76, f32[1569]{0:T(1024)S(1)} %fusion.107, f32[1569]{0:T(1024)S(1)} %broadcast_multiply_fusion, f32[1568,768]{1,0:T(8,128)S(1)} %bitcast_add_fusion.2, ...), kind=kOutput, calls=%fused_computation.83 | convolution fusion | flops 3710145024 | bytes 12017928 | tf_op jit(solution)/shard_map/td,tf->df/dot_general | solution.py:280
  227.5 5.3 convolution_convert_fusion.2
  232.7 4.8 convolution_convert_fusion
  244.3 5.4 convolution_convert_fusion.3
  251.6 16.8 %collective-permute-done.48 = bf16[4,2,48,1536]{3,2,0,1:T(8,128)(2,1)} collective-permute-done((bf16[4,2,48,1536]{3,2,0,1:T(8,128)(2,1)}, bf16[4,2,48,1536]{3,2,0,1:T(8,128)(2,1)}, u32[]{:S(2)}, u32[]{:S(2)}) %collective-permute-start.48) | collective-permute-done | bytes 1179680 | tf_op jit(solution)/shard_map/ppermute | solution.py:48
  273.7 11.4 %collective-permute-done.49 = bf16[4,48,1536]{2,1,0:T(8,128)(2,1)S(1)} collective-permute-done((bf16[4,48,1536]{2,1,0:T(8,128)(2,1)S(1)}, bf16[4,48,1536]{2,1,0:T(8,128)(2,1)S(1)}, u32[]{:S(2)}, u32[]{:S(2)}) %collective-permute-start.49) | collective-permute-done | bytes 589856 | tf_op jit(solution)/shard_map/ppermute | solution.py:48
  294.6 4.4 collective-permute-start.51
  303.4 5.0 collective-permute-start.52
  309.2 5.9 collective-permute-start.44
  317.8 5.4 collective-permute-done.55
  326.0 4.8 multiply_reduce_fusion.2
  330.8 6.8 fusion.124
  356.4 10.0 %multiply_reduce_fusion = (f32[8,6,197]{2,1,0:T(8,128)S(1)}, f32[8,6,197,197]{2,3,1,0:T(8,128)}) fusion(f32[8,6,197,197]{2,3,1,0:T(8,128)} %copy-done.2, f32[8,6,197]{2,1,0:T(8,128)S(1)} %copy-done.29, bf16[8,197,6,64]{1,3,2,0:T(8,128)(2,1)S(1)} %copy.290, f32[8,197,6,64]{1,3,2,0:T(8,128)} %bitcast.457, f32[6,64]{1,0:T(8,128)S(1)} %copy-done.66), kind=kOutput, calls=%fused_computation.3 | convolution fusion | flops 245231904 | bytes 18610944 | tf_op jit(solution)/shard_map/bihe,bjhe->bhij/dot_general | solution.py:123
  366.4 11.3 %multiply_convert_fusion = bf16[8,6,197,197]{2,3,1,0:T(8,128)(2,1)} fusion(f32[8,6,197,197]{2,3,1,0:T(8,128)} %get-tuple-element.205, f32[8,6,197,197]{2,3,1,0:T(8,128)} %copy-done.2, f32[8,6,197]{2,1,0:T(8,128)S(1)} %get-tuple-element.204, f32[8,6,197]{2,1,0:T(8,128)S(1)} %copy-done.29), kind=kLoop, calls=%fused_computation.2 | loop fusion | flops 7451328 | bytes 18703968 | tf_op jit(solution)/shard_map/convert_element_type | solution.py:125
  377.7 5.3 fusion.132
  383.1 5.3 convolution_convert_fusion.11
  399.2 7.6 %bitcast_convert_fusion.3 = bf16[768,3,384]{0,2,1:T(8,128)(2,1)S(1)} fusion(bf16[1,8,197,384]{3,2,0,1:T(8,128)(2,1)} %copy.297, bf16[1,8,197,384]{3,2,0,1:T(8,128)(2,1)} %copy.296, bf16[1,8,197,384]{3,2,0,1:T(8,128)(2,1)} %copy.295, f32[768]{0:T(1024)S(1)} %copy-done.101, f32[768]{0:T(1024)S(1)} %copy-done.55, f32[8,197]{1,0:T(8,128)S(1)} %copy-done.59, ...), kind=kOutput, calls=%fused_computation.81 | convolution fusion | flops 2807728128 | bytes 10260800 | tf_op jit(solution)/shard_map/bld,cblk->dck/dot_general | solution.py:136
  418.0 7.5 %bitcast_convert_fusion.1 = bf16[8,197,768]{2,1,0:T(8,128)(2,1)} fusion(bf16[768,3,384]{2,0,1:T(8,128)(2,1)} %param.36, bf16[1,8,197,384]{3,2,0,1:T(8,128)(2,1)} %copy.297, bf16[1,8,197,384]{3,2,0,1:T(8,128)(2,1)} %copy.296, bf16[1,8,197,384]{3,2,0,1:T(8,128)(2,1)} %copy.295), kind=kOutput, calls=%fused_computation.37 | convolution fusion | flops 2793529344 | bytes 7821312 | tf_op jit(solution)/shard_map/cblk,dck->bld/dot_general | solution.py:143
  434.3 7.0 collective-permute-done.33
  457.1 5.5 collective-permute-start.28
  473.0 4.8 fusion.119
  478.0 8.2 %multiply_reduce_fusion.3 = (bf16[768]{0:T(1024)(128)(2,1)S(1)}, f32[1576]{0:T(1024)S(1)}, f32[1576,768]{1,0:T(8,128)}) fusion(f32[1576,768]{1,0:T(8,128)} %concatenate.55, f32[1576]{0:T(1024)S(1)} %get-tuple-element.200, f32[1576]{0:T(1024)S(1)} %copy-done.43, bf16[1576,768]{1,0:T(8,128)(2,1)} %collective-permute-done.5, ...), kind=kLoop, calls=%fused_computation.54 | loop fusion | flops 15732440 | bytes 14554240 | tf_op jit(solution)/shard_map/transpose(jvp())/reduce_sum | solution.py:14
  486.3 5.3 reshape.612
  491.7 4.9 fusion.9
  507.4 4.4 convolution_convert_fusion.13
  511.8 4.1 convolution_convert_fusion.7
  516.0 4.7 reshape.614
  520.7 6.2 fusion.36
  533.0 5.1 fusion.130
  541.0 4.3 copy.304
  547.8 4.4 copy.307
  554.7 5.5 fusion.131
  560.2 4.4 copy.310
  569.3 4.1 copy.348
  573.4 8.2 %reshape.673 = bf16[1152,8,196]{0,2,1:T(8,128)(2,1)} reshape(bf16[3,384,8,196]{1,0,3,2:T(4,128)(2,1)} %copy.348) | data formatting | bytes 7225344 | tf_op jit(solution)/shard_map/pfd,cfkp->dck/dot_general | solution.py:188
  581.7 8.9 %fusion.22 = bf16[768,1152]{1,0:T(8,128)(2,1)S(1)} fusion(bf16[1152,8,196]{0,2,1:T(8,128)(2,1)} %reshape.673, f32[196,8,768]{2,1,0:T(8,128)} %get-tuple-element.142, f32[768]{0:T(1024)S(1)} %copy-done.84, f32[768]{0:T(1024)S(1)} %copy-done.53, f32[196,8]{0,1:T(8,128)S(1)} %copy-done.62, f32[196,8]{0,1:T(8,128)S(1)} %copy-done.64), kind=kOutput, calls=%fused_computation.86 | convolution fusion | flops 2781437952 | bytes 10217728 | tf_op jit(solution)/shard_map/pfd,cfkp->dck/dot_general | solution.py:188
  598.9 14.2 %collective-permute-done.16 = bf16[4,2,48,1152]{3,2,0,1:T(8,128)(2,1)S(1)} collective-permute-done((bf16[4,2,48,1152]{3,2,0,1:T(8,128)(2,1)S(1)}, bf16[4,2,48,1152]{3,2,0,1:T(8,128)(2,1)S(1)}, u32[]{:S(2)}, u32[]{:S(2)}) %collective-permute-start.16) | collective-permute-done | bytes 884768 | tf_op jit(solution)/shard_map/ppermute | solution.py:48
  617.8 7.4 %collective-permute-done.17 = bf16[4,48,1152]{2,1,0:T(8,128)(2,1)S(1)} collective-permute-done((bf16[4,48,1152]{2,1,0:T(8,128)(2,1)S(1)}, bf16[4,48,1152]{2,1,0:T(8,128)(2,1)S(1)}, u32[]{:S(2)}, u32[]{:S(2)}) %collective-permute-start.17) | collective-permute-done | bytes 442400 | tf_op jit(solution)/shard_map/ppermute | solution.py:48
  641.0 5.2 multiply_reduce_fusion.7
  648.4 4.9 collective-permute-start.20
  654.7 6.3 collective-permute-done.8
  662.4 6.2 collective-permute-done.9
  668.8 4.3 collective-permute-start.10
  673.1 6.1 fusion.123
  684.5 5.3 collective-permute-start.12
  693.2 4.3 collective-permute-done.15
  (536 shorter events, 285.0 us)
Async XLA Ops:
  0.7 177.7 %copy-start = (bf16[768,1536]{1,0:T(8,128)(2,1)S(1)}, bf16[768,1536]{1,0:T(8,128)(2,1)}, u32[]{:S(2)}) copy-start(bf16[768,1536]{1,0:T(8,128)(2,1)} %param.42) | copy-start | bytes 7077892
  82.3 3.3 collective-permute-start
  90.1 5.0 collective-permute-start.1
  104.6 46.2 %copy-start.41 = (f32[8,197]{1,0:T(8,128)}, f32[8,197]{1,0:T(8,128)S(1)}, u32[]{:S(2)}) copy-start(f32[8,197]{1,0:T(8,128)S(1)} %broadcast_multiply_fusion.1) | copy-start | bytes 18916
  144.4 12.8 %collective-permute-start.2 = (bf16[1576,768]{1,0:T(8,128)(2,1)}, bf16[1576,768]{1,0:T(8,128)(2,1)}, u32[]{:S(2)}, u32[]{:S(2)}) collective-permute-start(bf16[1576,768]{1,0:T(8,128)(2,1)} %convolution_convert_fusion.4), channel_id=1, source_target_pairs={{0,1},{1,0},{2,3},{3,2},{4,5},{5,4},{6,7},{7,6},{8,9},{9,8},{10,11... | collective-permute-start | bytes 7262216 | tf_op jit(solution)/shard_map/ppermute | solution.py:32
  176.1 43.6 %copy-start.4 = (f32[1568,768]{1,0:T(8,128)}, f32[1568,768]{1,0:T(8,128)S(1)}, u32[]{:S(2)}) copy-start(f32[1568,768]{1,0:T(8,128)S(1)} %bitcast_add_fusion.2) | copy-start | bytes 14450692
  178.4 41.2 %copy-start.44 = (f32[1569]{0:T(1024)}, f32[1569]{0:T(1024)S(1)}, u32[]{:S(2)}) copy-start(f32[1569]{0:T(1024)S(1)} %fusion.107) | copy-start | bytes 18832
  238.9 29.5 %collective-permute-start.48 = (bf16[4,2,48,1536]{3,2,0,1:T(8,128)(2,1)}, bf16[4,2,48,1536]{3,2,0,1:T(8,128)(2,1)}, u32[]{:S(2)}, u32[]{:S(2)}) collective-permute-start(bf16[4,2,48,1536]{3,2,0,1:T(8,128)(2,1)} %bitcast.430), channel_id=1, source_target_pairs={{0,4},{2,6},{4,0},{6,2},{8,12},{10,14},{12,8},{14,10},{16,20},{18,... | collective-permute-start | bytes 3538952 | tf_op jit(solution)/shard_map/ppermute | solution.py:48
  242.8 28.9 %collective-permute-start.40 = (bf16[4,2,48,1536]{3,2,0,1:T(8,128)(2,1)}, bf16[4,2,48,1536]{3,2,0,1:T(8,128)(2,1)S(1)}, u32[]{:S(2)}, u32[]{:S(2)}) collective-permute-start(bf16[4,2,48,1536]{3,2,0,1:T(8,128)(2,1)} %bitcast.431), channel_id=1, source_target_pairs={{0,2},{2,0},{4,6},{6,4},{8,10},{10,8},{12,14},{14,12},{16,18},{18,... | collective-permute-start | bytes 3538952 | tf_op jit(solution)/shard_map/ppermute | solution.py:48
  249.7 76.2 %collective-permute-start.4 = (bf16[1569,768]{1,0:T(8,128)(2,1)}, bf16[1569,768]{1,0:T(8,128)(2,1)}, u32[]{:S(2)}, u32[]{:S(2)}) collective-permute-start(bf16[1569,768]{1,0:T(8,128)(2,1)} %convolution_convert_fusion.2), channel_id=1, source_target_pairs={{0,1},{1,0},{2,3},{3,2},{4,5},{5,4},{6,7},{7,6},{8,9},{9,8},{10,11... | collective-permute-start | bytes 7229960 | tf_op jit(solution)/shard_map/ppermute | solution.py:32
  249.7 81.1 %collective-permute-start.3 = (bf16[1569,768]{1,0:T(8,128)(2,1)}, bf16[1569,768]{1,0:T(8,128)(2,1)}, u32[]{:S(2)}, u32[]{:S(2)}) collective-permute-start(bf16[1569,768]{1,0:T(8,128)(2,1)} %convolution_convert_fusion.3), channel_id=1, source_target_pairs={{0,1},{1,0},{2,3},{3,2},{4,5},{5,4},{6,7},{7,6},{8,9},{9,8},{10,11... | collective-permute-start | bytes 7229960 | tf_op jit(solution)/shard_map/ppermute | solution.py:32
  269.9 56.0 %slice-start.5 = ((s8[4816896]{0:T(1024)(128)(4,1)}), s8[4194304]{0:T(1024)(128)(4,1)S(1)}, s32[]{:S(2)}) async-start(s8[4816896]{0:T(1024)(128)(4,1)} %bitcast.440), calls=%async_computation.5 | async-start | bytes 8388608
  270.0 15.1 %collective-permute-start.49 = (bf16[4,48,1536]{2,1,0:T(8,128)(2,1)S(1)}, bf16[4,48,1536]{2,1,0:T(8,128)(2,1)S(1)}, u32[]{:S(2)}, u32[]{:S(2)}) collective-permute-start(bf16[4,48,1536]{2,1,0:T(8,128)(2,1)S(1)} %dynamic-slice_bitcast_fusion), channel_id=1, source_target_pairs={{0,2},{2,0},{4,6},{6,4},{8,10},{10,8},{12,14},{14,12},{16,18},{18,... | collective-permute-start | bytes 1769480 | tf_op jit(solution)/shard_map/ppermute | solution.py:48
  272.1 53.8 %copy-start.45 = (f32[1569]{0:T(1024)S(1)}, f32[1569]{0:T(1024)}, u32[]{:S(2)}) copy-start(f32[1569]{0:T(1024)} %copy-done.44) | copy-start | bytes 18832
  272.1 17.5 %collective-permute-start.41 = (bf16[4,48,1536]{2,1,0:T(8,128)(2,1)S(1)}, bf16[4,48,1536]{2,1,0:T(8,128)(2,1)S(1)}, u32[]{:S(2)}, u32[]{:S(2)}) collective-permute-start(bf16[4,48,1536]{2,1,0:T(8,128)(2,1)S(1)} %dynamic-slice_bitcast_fusion.1), channel_id=1, source_target_pairs={{0,4},{2,6},{4,0},{6,2},{8,12},{10,14},{12,8},{14,10},{16,20},{18,... | collective-permute-start | bytes 1769480 | tf_op jit(solution)/shard_map/ppermute | solution.py:48
  285.3 7.7 %collective-permute-start.50 = (bf16[48,1536]{1,0:T(8,128)(2,1)S(1)}, bf16[48,1536]{1,0:T(8,128)(2,1)S(1)}, u32[]{:S(2)}, u32[]{:S(2)}) collective-permute-start(bf16[48,1536]{1,0:T(8,128)(2,1)S(1)} %get-tuple-element.155), channel_id=1, source_target_pairs={{0,8},{2,10},{4,12},{6,14},{1,9},{3,11},{5,13},{7,15}} | collective-permute-start | bytes 442376 | tf_op jit(solution)/shard_map/ppermute | solution.py:62
  288.9 10.1 %collective-permute-start.53 = (bf16[48,1536]{1,0:T(8,128)(2,1)S(1)}, bf16[48,1536]{1,0:T(8,128)(2,1)S(1)}, u32[]{:S(2)}, u32[]{:S(2)}) collective-permute-start(bf16[48,1536]{1,0:T(8,128)(2,1)S(1)} %get-tuple-element.156), channel_id=1, source_target_pairs={{24,16},{26,18},{28,20},{30,22},{25,17},{27,19},{29,21},{31,23}} | collective-permute-start | bytes 442376 | tf_op jit(solution)/shard_map/ppermute | solution.py:63
  289.8 4.8 collective-permute-start.42
  293.0 10.4 %collective-permute-start.45 = (bf16[48,1536]{1,0:T(8,128)(2,1)S(1)}, bf16[48,1536]{1,0:T(8,128)(2,1)S(1)}, u32[]{:S(2)}, u32[]{:S(2)}) collective-permute-start(bf16[48,1536]{1,0:T(8,128)(2,1)S(1)} %get-tuple-element.160), channel_id=1, source_target_pairs={{24,16},{26,18},{28,20},{30,22},{25,17},{27,19},{29,21},{31,23}} | collective-permute-start | bytes 442376 | tf_op jit(solution)/shard_map/ppermute | solution.py:63
  294.6 8.0 %collective-permute-start.51 = (bf16[48,1536]{1,0:T(8,128)(2,1)S(1)}, bf16[48,1536]{1,0:T(8,128)(2,1)S(1)}, u32[]{:S(2)}, u32[]{:S(2)}) collective-permute-start(bf16[48,1536]{1,0:T(8,128)(2,1)S(1)} %fusion.74), channel_id=1, source_target_pairs={{0,8},{2,10},{4,12},{6,14},{8,16},{10,18},{12,20},{14,22},{1,9},{3... | collective-permute-start | bytes 442376 | tf_op jit(solution)/shard_map/ppermute | solution.py:62
  299.1 9.3 %collective-permute-start.43 = (bf16[48,1536]{1,0:T(8,128)(2,1)S(1)}, bf16[48,1536]{1,0:T(8,128)(2,1)S(1)}, u32[]{:S(2)}, u32[]{:S(2)}) collective-permute-start(bf16[48,1536]{1,0:T(8,128)(2,1)S(1)} %fusion.80), channel_id=1, source_target_pairs={{0,8},{2,10},{4,12},{6,14},{8,16},{10,18},{12,20},{14,22},{1,9},{3... | collective-permute-start | bytes 442376 | tf_op jit(solution)/shard_map/ppermute | solution.py:62
  302.7 6.5 collective-permute-start.54
  303.4 13.1 %collective-permute-start.52 = (bf16[48,1536]{1,0:T(8,128)(2,1)S(1)}, bf16[48,1536]{1,0:T(8,128)(2,1)S(1)}, u32[]{:S(2)}, u32[]{:S(2)}) collective-permute-start(bf16[48,1536]{1,0:T(8,128)(2,1)S(1)} %get-tuple-element.153), channel_id=1, source_target_pairs={{0,8},{2,10},{4,12},{6,14},{8,16},{10,18},{12,20},{14,22},{16,24},... | collective-permute-start | bytes 442376 | tf_op jit(solution)/shard_map/ppermute | solution.py:62
  308.5 6.6 collective-permute-start.46
  309.2 14.8 %collective-permute-start.44 = (bf16[48,1536]{1,0:T(8,128)(2,1)S(1)}, bf16[48,1536]{1,0:T(8,128)(2,1)S(1)}, u32[]{:S(2)}, u32[]{:S(2)}) collective-permute-start(bf16[48,1536]{1,0:T(8,128)(2,1)S(1)} %get-tuple-element.157), channel_id=1, source_target_pairs={{0,8},{2,10},{4,12},{6,14},{8,16},{10,18},{12,20},{14,22},{16,24},... | collective-permute-start | bytes 442376 | tf_op jit(solution)/shard_map/ppermute | solution.py:62
  315.1 8.1 %collective-permute-start.55 = (bf16[48,1536]{1,0:T(8,128)(2,1)S(1)}, bf16[48,1536]{1,0:T(8,128)(2,1)S(1)}, u32[]{:S(2)}, u32[]{:S(2)}) collective-permute-start(bf16[48,1536]{1,0:T(8,128)(2,1)S(1)} %fusion.73), channel_id=1, source_target_pairs={{8,0},{10,2},{12,4},{14,6},{16,8},{18,10},{20,12},{22,14},{24,16},... | collective-permute-start | bytes 442376 | tf_op jit(solution)/shard_map/ppermute | solution.py:63
  316.5 8.7 %collective-permute-start.47 = (bf16[48,1536]{1,0:T(8,128)(2,1)S(1)}, bf16[48,1536]{1,0:T(8,128)(2,1)S(1)}, u32[]{:S(2)}, u32[]{:S(2)}) collective-permute-start(bf16[48,1536]{1,0:T(8,128)(2,1)S(1)} %fusion.79), channel_id=1, source_target_pairs={{8,0},{10,2},{12,4},{14,6},{16,8},{18,10},{20,12},{22,14},{24,16},... | collective-permute-start | bytes 442376 | tf_op jit(solution)/shard_map/ppermute | solution.py:63
  412.9 19.6 %collective-permute-start.24 = (bf16[4,2,48,768]{3,2,1,0:T(8,128)(2,1)}, bf16[4,2,48,768]{3,2,1,0:T(8,128)(2,1)}, u32[]{:S(2)}, u32[]{:S(2)}) collective-permute-start(bf16[4,2,48,768]{3,2,1,0:T(8,128)(2,1)} %dynamic-slice_bitcast_fusion.2), channel_id=1, source_target_pairs={{0,2},{2,0},{4,6},{6,4},{8,10},{10,8},{12,14},{14,12},{16,18},{18,... | collective-permute-start | bytes 1769480 | tf_op jit(solution)/shard_map/ppermute | solution.py:48
  416.5 15.2 %collective-permute-start.32 = (bf16[4,2,48,768]{3,2,0,1:T(8,128)(2,1)S(1)}, bf16[4,2,48,768]{3,2,0,1:T(8,128)(2,1)S(1)}, u32[]{:S(2)}, u32[]{:S(2)}) collective-permute-start(bf16[4,2,48,768]{3,2,0,1:T(8,128)(2,1)S(1)} %bitcast.480), channel_id=1, source_target_pairs={{0,4},{2,6},{4,0},{6,2},{8,12},{10,14},{12,8},{14,10},{16,20},{18,... | collective-permute-start | bytes 1769480 | tf_op jit(solution)/shard_map/ppermute | solution.py:48
  429.4 43.5 %copy-start.43 = (f32[1576]{0:T(1024)S(1)}, f32[1576]{0:T(1024)}, u32[]{:S(2)}) copy-start(f32[1576]{0:T(1024)} %div.138) | copy-start | bytes 18916
  429.4 43.5 %collective-permute-start.5 = (bf16[1576,768]{1,0:T(8,128)(2,1)}, bf16[1576,768]{1,0:T(8,128)(2,1)}, u32[]{:S(2)}, u32[]{:S(2)}) collective-permute-start(bf16[1576,768]{1,0:T(8,128)(2,1)} %convert_element_type.945), channel_id=1, source_target_pairs={{0,1},{1,0},{2,3},{3,2},{4,5},{5,4},{6,7},{7,6},{8,9},{9,8},{10,11... | collective-permute-start | bytes 7262216 | tf_op jit(solution)/shard_map/ppermute | solution.py:32
  431.6 41.3 %copy-start.11 = (bf16[1576,768]{1,0:T(8,128)(2,1)S(1)}, bf16[1576,768]{1,0:T(8,128)(2,1)}, u32[]{:S(2)}) copy-start(bf16[1576,768]{1,0:T(8,128)(2,1)} %convert_element_type.945) | copy-start | bytes 7262212
  431.8 9.5 %collective-permute-start.33 = (bf16[4,48,768]{2,1,0:T(8,128)(2,1)S(1)}, bf16[4,48,768]{2,1,0:T(8,128)(2,1)S(1)}, u32[]{:S(2)}, u32[]{:S(2)}) collective-permute-start(bf16[4,48,768]{2,1,0:T(8,128)(2,1)S(1)} %dynamic-slice_bitcast_fusion.5), channel_id=1, source_target_pairs={{0,2},{2,0},{4,6},{6,4},{8,10},{10,8},{12,14},{14,12},{16,18},{18,... | collective-permute-start | bytes 884744 | tf_op jit(solution)/shard_map/ppermute | solution.py:48
  433.7 11.6 %collective-permute-start.25 = (bf16[4,48,768]{2,1,0:T(8,128)(2,1)S(1)}, bf16[4,48,768]{2,1,0:T(8,128)(2,1)S(1)}, u32[]{:S(2)}, u32[]{:S(2)}) collective-permute-start(bf16[4,48,768]{2,1,0:T(8,128)(2,1)S(1)} %dynamic-slice_bitcast_fusion.6), channel_id=1, source_target_pairs={{0,4},{2,6},{4,0},{6,2},{8,12},{10,14},{12,8},{14,10},{16,20},{18,... | collective-permute-start | bytes 884744 | tf_op jit(solution)/shard_map/ppermute | solution.py:48
  441.4 7.1 %collective-permute-start.34 = (bf16[48,768]{1,0:T(8,128)(2,1)S(1)}, bf16[48,768]{1,0:T(8,128)(2,1)S(1)}, u32[]{:S(2)}, u32[]{:S(2)}) collective-permute-start(bf16[48,768]{1,0:T(8,128)(2,1)S(1)} %get-tuple-element.177), channel_id=1, source_target_pairs={{0,8},{2,10},{4,12},{6,14},{1,9},{3,11},{5,13},{7,15}} | collective-permute-start | bytes 221192 | tf_op jit(solution)/shard_map/ppermute | solution.py:62
  445.5 6.5 collective-permute-start.26
  447.2 8.2 %collective-permute-start.29 = (bf16[48,768]{1,0:T(8,128)(2,1)S(1)}, bf16[48,768]{1,0:T(8,128)(2,1)S(1)}, u32[]{:S(2)}, u32[]{:S(2)}) collective-permute-start(bf16[48,768]{1,0:T(8,128)(2,1)S(1)} %get-tuple-element.174), channel_id=1, source_target_pairs={{24,16},{26,18},{28,20},{30,22},{25,17},{27,19},{29,21},{31,23}} | collective-permute-start | bytes 221192 | tf_op jit(solution)/shard_map/ppermute | solution.py:63
  447.8 6.6 collective-permute-start.37
  448.5 5.9 collective-permute-start.35
  452.0 4.4 collective-permute-start.27
  454.5 12.1 %collective-permute-start.38 = (bf16[48,768]{1,0:T(8,128)(2,1)S(1)}, bf16[48,768]{1,0:T(8,128)(2,1)S(1)}, u32[]{:S(2)}, u32[]{:S(2)}) collective-permute-start(bf16[48,768]{1,0:T(8,128)(2,1)S(1)} %get-tuple-element.176), channel_id=1, source_target_pairs={{16,8},{18,10},{20,12},{22,14},{24,16},{26,18},{28,20},{30,22},{17... | collective-permute-start | bytes 221192 | tf_op jit(solution)/shard_map/ppermute | solution.py:63
  456.5 11.5 %collective-permute-start.30 = (bf16[48,768]{1,0:T(8,128)(2,1)S(1)}, bf16[48,768]{1,0:T(8,128)(2,1)S(1)}, u32[]{:S(2)}, u32[]{:S(2)}) collective-permute-start(bf16[48,768]{1,0:T(8,128)(2,1)S(1)} %get-tuple-element.172), channel_id=1, source_target_pairs={{16,8},{18,10},{20,12},{22,14},{24,16},{26,18},{28,20},{30,22},{17... | collective-permute-start | bytes 221192 | tf_op jit(solution)/shard_map/ppermute | solution.py:63
  457.1 46.7 %collective-permute-start.28 = (bf16[48,768]{1,0:T(8,128)(2,1)S(1)}, bf16[48,768]{1,0:T(8,128)(2,1)}, u32[]{:S(2)}, u32[]{:S(2)}) collective-permute-start(bf16[48,768]{1,0:T(8,128)(2,1)S(1)} %get-tuple-element.171), channel_id=1, source_target_pairs={{0,8},{2,10},{4,12},{6,14},{8,16},{10,18},{12,20},{14,22},{16,24},... | collective-permute-start | bytes 221192 | tf_op jit(solution)/shard_map/ppermute | solution.py:62
  462.7 6.6 collective-permute-start.36
  466.6 6.2 collective-permute-start.39
  468.0 35.9 %collective-permute-start.31 = (bf16[48,768]{1,0:T(8,128)(2,1)S(1)}, bf16[48,768]{1,0:T(8,128)(2,1)S(1)}, u32[]{:S(2)}, u32[]{:S(2)}) collective-permute-start(bf16[48,768]{1,0:T(8,128)(2,1)S(1)} %fusion.100), channel_id=1, source_target_pairs={{8,0},{10,2},{12,4},{14,6},{16,8},{18,10},{20,12},{22,14},{24,16},... | collective-permute-start | bytes 221192 | tf_op jit(solution)/shard_map/ppermute | solution.py:63
  503.2 8.6 %collective-permute-start.6 = (bf16[1568,384]{1,0:T(8,128)(2,1)S(1)}, bf16[1568,384]{1,0:T(8,128)(2,1)}, u32[]{:S(2)}, u32[]{:S(2)}) collective-permute-start(bf16[1568,384]{1,0:T(8,128)(2,1)S(1)} %convolution_convert_fusion.8), channel_id=1, source_target_pairs={{0,1},{1,0},{2,3},{3,2},{4,5},{5,4},{6,7},{7,6},{8,9},{9,8},{10,11... | collective-permute-start | bytes 3612680 | tf_op jit(solution)/shard_map/ppermute | solution.py:32
  590.9 22.1 %collective-permute-start.16 = (bf16[4,2,48,1152]{3,2,0,1:T(8,128)(2,1)S(1)}, bf16[4,2,48,1152]{3,2,0,1:T(8,128)(2,1)S(1)}, u32[]{:S(2)}, u32[]{:S(2)}) collective-permute-start(bf16[4,2,48,1152]{3,2,0,1:T(8,128)(2,1)S(1)} %bitcast.478), channel_id=1, source_target_pairs={{0,2},{2,0},{4,6},{6,4},{8,10},{10,8},{12,14},{14,12},{16,18},{18,... | collective-permute-start | bytes 2654216 | tf_op jit(solution)/shard_map/ppermute | solution.py:48
  598.4 42.6 %collective-permute-start.7 = (bf16[1568,768]{1,0:T(8,128)(2,1)}, bf16[1568,768]{1,0:T(8,128)(2,1)}, u32[]{:S(2)}, u32[]{:S(2)}) collective-permute-start(bf16[1568,768]{1,0:T(8,128)(2,1)} %bitcast.429), channel_id=1, source_target_pairs={{0,1},{1,0},{2,3},{3,2},{4,5},{5,4},{6,7},{7,6},{8,9},{9,8},{10,11... | collective-permute-start | bytes 7225352 | tf_op jit(solution)/shard_map/ppermute | solution.py:32
  613.3 11.9 %collective-permute-start.17 = (bf16[4,48,1152]{2,1,0:T(8,128)(2,1)S(1)}, bf16[4,48,1152]{2,1,0:T(8,128)(2,1)S(1)}, u32[]{:S(2)}, u32[]{:S(2)}) collective-permute-start(bf16[4,48,1152]{2,1,0:T(8,128)(2,1)S(1)} %dynamic-slice_bitcast_fusion.3), channel_id=1, source_target_pairs={{0,4},{2,6},{4,0},{6,2},{8,12},{10,14},{12,8},{14,10},{16,20},{18,... | collective-permute-start | bytes 1327112 | tf_op jit(solution)/shard_map/ppermute | solution.py:48
  625.4 9.3 %collective-permute-start.18 = (bf16[48,1152]{1,0:T(8,128)(2,1)S(1)}, bf16[48,1152]{1,0:T(8,128)(2,1)S(1)}, u32[]{:S(2)}, u32[]{:S(2)}) collective-permute-start(bf16[48,1152]{1,0:T(8,128)(2,1)S(1)} %get-tuple-element.163), channel_id=1, source_target_pairs={{0,8},{2,10},{4,12},{6,14},{1,9},{3,11},{5,13},{7,15}} | collective-permute-start | bytes 331784 | tf_op jit(solution)/shard_map/ppermute | solution.py:62
  633.3 5.7 collective-permute-start.21
  635.3 3.9 collective-permute-start.19
  640.3 13.0 %collective-permute-start.22 = (bf16[48,1152]{1,0:T(8,128)(2,1)S(1)}, bf16[48,1152]{1,0:T(8,128)(2,1)S(1)}, u32[]{:S(2)}, u32[]{:S(2)}) collective-permute-start(bf16[48,1152]{1,0:T(8,128)(2,1)S(1)} %get-tuple-element.162), channel_id=1, source_target_pairs={{16,8},{18,10},{20,12},{22,14},{24,16},{26,18},{28,20},{30,22},{17... | collective-permute-start | bytes 331784 | tf_op jit(solution)/shard_map/ppermute | solution.py:63
  647.0 13.9 %collective-permute-start.8 = (bf16[4,2,49,768]{3,0,2,1:T(4,128)(2,1)S(1)}, bf16[4,2,49,768]{3,0,2,1:T(4,128)(2,1)S(1)}, u32[]{:S(2)}, u32[]{:S(2)}) collective-permute-start(bf16[4,2,49,768]{3,0,2,1:T(4,128)(2,1)S(1)} %copy.318), channel_id=1, source_target_pairs={{0,4},{2,6},{4,0},{6,2},{8,12},{10,14},{12,8},{14,10},{16,20},{18,... | collective-permute-start | bytes 1806344 | tf_op jit(solution)/shard_map/ppermute | solution.py:48
  648.4 13.3 %collective-permute-start.20 = (bf16[48,1152]{1,0:T(8,128)(2,1)S(1)}, bf16[48,1152]{1,0:T(8,128)(2,1)S(1)}, u32[]{:S(2)}, u32[]{:S(2)}) collective-permute-start(bf16[48,1152]{1,0:T(8,128)(2,1)S(1)} %get-tuple-element.161), channel_id=1, source_target_pairs={{0,8},{2,10},{4,12},{6,14},{8,16},{10,18},{12,20},{14,22},{16,24},... | collective-permute-start | bytes 331784 | tf_op jit(solution)/shard_map/ppermute | solution.py:62
  653.4 8.3 %collective-permute-start.23 = (bf16[48,1152]{1,0:T(8,128)(2,1)S(1)}, bf16[48,1152]{1,0:T(8,128)(2,1)S(1)}, u32[]{:S(2)}, u32[]{:S(2)}) collective-permute-start(bf16[48,1152]{1,0:T(8,128)(2,1)S(1)} %fusion.84), channel_id=1, source_target_pairs={{8,0},{10,2},{12,4},{14,6},{16,8},{18,10},{20,12},{22,14},{24,16},... | collective-permute-start | bytes 331784 | tf_op jit(solution)/shard_map/ppermute | solution.py:63
  661.1 7.5 %collective-permute-start.9 = (bf16[4,49,768]{2,1,0:T(8,128)(2,1)S(1)}, bf16[4,49,768]{2,1,0:T(8,128)(2,1)S(1)}, u32[]{:S(2)}, u32[]{:S(2)}) collective-permute-start(bf16[4,49,768]{2,1,0:T(8,128)(2,1)S(1)} %dynamic-slice_bitcast_fusion.4), channel_id=1, source_target_pairs={{0,2},{2,0},{4,6},{6,4},{8,10},{10,8},{12,14},{14,12},{16,18},{18,... | collective-permute-start | bytes 903176 | tf_op jit(solution)/shard_map/ppermute | solution.py:48
  668.8 11.1 %collective-permute-start.10 = (bf16[49,768]{1,0:T(8,128)(2,1)S(1)}, bf16[49,768]{1,0:T(8,128)(2,1)S(1)}, u32[]{:S(2)}, u32[]{:S(2)}) collective-permute-start(bf16[49,768]{1,0:T(8,128)(2,1)S(1)} %get-tuple-element.169), channel_id=1, source_target_pairs={{0,8},{2,10},{4,12},{6,14},{1,9},{3,11},{5,13},{7,15}} | collective-permute-start | bytes 225800 | tf_op jit(solution)/shard_map/ppermute | solution.py:62
  679.2 2.0 collective-permute-start.13
  679.9 3.4 collective-permute-start.11
  683.3 6.5 collective-permute-start.14
  684.5 8.7 %collective-permute-start.12 = (bf16[49,768]{1,0:T(8,128)(2,1)S(1)}, bf16[49,768]{1,0:T(8,128)(2,1)S(1)}, u32[]{:S(2)}, u32[]{:S(2)}) collective-permute-start(bf16[49,768]{1,0:T(8,128)(2,1)S(1)} %get-tuple-element.167), channel_id=1, source_target_pairs={{0,8},{2,10},{4,12},{6,14},{8,16},{10,18},{12,20},{14,22},{16,24},... | collective-permute-start | bytes 225800 | tf_op jit(solution)/shard_map/ppermute | solution.py:62
  689.9 7.6 %collective-permute-start.15 = (bf16[49,768]{1,0:T(8,128)(2,1)S(1)}, bf16[49,768]{1,0:T(8,128)(2,1)S(1)}, u32[]{:S(2)}, u32[]{:S(2)}) collective-permute-start(bf16[49,768]{1,0:T(8,128)(2,1)S(1)} %fusion.90), channel_id=1, source_target_pairs={{8,0},{10,2},{12,4},{14,6},{16,8},{18,10},{20,12},{22,14},{24,16},... | collective-permute-start | bytes 225800 | tf_op jit(solution)/shard_map/ppermute | solution.py:63
  (108 other events, 863.8 us)

commit v2 on v1

v2 whole, which is shorter than its diff:
```python
import functools

import jax
import jax.numpy as jnp
from jax import lax
from jax.experimental import pallas as pl
from jax.experimental.pallas import tpu as pltpu
from jax.sharding import PartitionSpec as P

HEAD = 64
FRAMES = 8
PLACES = 196
BLOCK = 16
ROWS = 208
BLOCKS = ROWS // BLOCK
PAIR = 2
EPS = 1e-06
LOW = jnp.bfloat16
VMEM_BYTES = 56 * 1024 * 1024


def dot(left, right):
    return jnp.dot(left, right, preferred_element_type=jnp.float32)


def dot_last(left, right):
    return lax.dot_general(left, right, (((1,), (1,)), ((), ())), preferred_element_type=jnp.float32)


def normed(field):
    center = field - jnp.mean(field, axis=-1, keepdims=True)
    spread_sq = jnp.mean(center * center, axis=-1, keepdims=True)
    inverse = lax.rsqrt(spread_sq + EPS)
    return center * inverse, inverse


def normed_back(unit, inverse, grad_unit):
    first = jnp.mean(grad_unit, axis=-1, keepdims=True)
    second = jnp.mean(grad_unit * unit, axis=-1, keepdims=True)
    return (grad_unit - first - unit * second) * inverse


def flat(field):
    return field.reshape((field.shape[0] * field.shape[1],) + field.shape[2:])


def wide(field):
    return field.astype(jnp.float32)


def iota(shape, axis):
    return lax.broadcasted_iota(jnp.int32, shape, axis)


def column_sum(field):
    return jnp.sum(field, axis=0, keepdims=True)


def call(kernel, grid, in_specs, out_specs, out_shapes, scratch, flops, args):
    moved = sum(a.size * a.dtype.itemsize for a in args) + sum(o.size * o.dtype.itemsize for o in out_shapes)
    return pl.pallas_call(
        kernel,
        grid=grid,
        in_specs=in_specs,
        out_specs=out_specs,
        out_shape=out_shapes,
        scratch_shapes=scratch,
        compiler_params=pltpu.CompilerParams(vmem_limit_bytes=VMEM_BYTES),
        cost_estimate=pl.CostEstimate(flops=int(flops), bytes_accessed=int(moved), transcendentals=0),
    )(*args)


def whole(array):
    zeros = (0,) * array.ndim
    return pl.BlockSpec(array.shape, lambda *at: zeros)


def shape(dims, kind=LOW):
    return jax.ShapeDtypeStruct(dims, kind)


def to_frames(rows, block):
    count = FRAMES * BLOCK
    at = iota((count, count + BLOCK), 0)
    source = 1 + FRAMES * (at % BLOCK) + at // BLOCK
    pick = jnp.where(source == iota((count, count + BLOCK), 1), 1.0, 0.0).astype(LOW)
    return dot(pick, rows)


def to_tokens(rows):
    count = FRAMES * BLOCK
    at = iota((count, count), 1)
    target = 1 + FRAMES * (at % BLOCK) + at // BLOCK
    pick = jnp.where(target == iota((count, count), 0), 1.0, 0.0).astype(LOW)
    return dot(pick, rows)


def fill_rows(source, tokens):
    count = tokens.shape[0]
    even = count // BLOCK * BLOCK
    source[0:even] = tokens[0:even]
    source[even:] = jnp.zeros((source.shape[0] - even, source.shape[1]), source.dtype)
    left = wide(tokens[even:count])
    tail = jnp.zeros((BLOCK, source.shape[1]), jnp.float32)
    for row in range(count - even):
        tail = tail + jnp.where(iota(tail.shape, 0) == row, left[row : row + 1], 0.0)
    source[even : even + BLOCK] = tail.astype(source.dtype)


def frame_rows(source, block, class_row, class_frames):
    count = FRAMES * BLOCK
    rows = to_frames(source[pl.ds(pl.multiple_of(block * count, count), count + BLOCK), :], block)
    at = iota((count, 1), 0)
    is_class = (block * BLOCK + at % BLOCK == PLACES) & (at // BLOCK < class_frames)
    return rows + jnp.where(is_class, class_row, 0.0)


def time_forward_kernel(
    clips, gain, shift, inproj, inbias, outproj, x_out, norm_out, qkv_out, probs_out, mixed_out, part_out, source
):
    half = outproj.shape[0]
    fill_rows(source, clips)
    class_row = wide(clips[0:1])

    def first(block, carry):
        rows = frame_rows(source, block, class_row, FRAMES)
        unit, _ = normed(rows)
        at = pl.ds(pl.multiple_of(block * BLOCK, BLOCK), BLOCK)
        x_out[:, at, :] = rows.astype(LOW).reshape(FRAMES, BLOCK, rows.shape[1])
        norm_out[:, at, :] = (unit * gain[...] + shift[...]).astype(LOW).reshape(FRAMES, BLOCK, rows.shape[1])
        return carry

    lax.fori_loop(0, BLOCKS, first, 0)

    def second(step, carry):
        at = pl.ds(step * PAIR, PAIR)
        linear = dot(flat(norm_out[at]), inproj[...])
        qkv_out[at] = heads_low(linear, inbias, half).reshape(PAIR, ROWS, 3 * half)
        return carry

    lax.fori_loop(0, FRAMES // PAIR, second, 0)
    count = FRAMES * BLOCK
    same = iota((count, count), 0) % BLOCK == iota((count, count), 1) % BLOCK

    def third(block, carry):
        at = pl.ds(pl.multiple_of(block * BLOCK, BLOCK), BLOCK)
        mixed = attend(flat(qkv_out[:, at, :]), same, lambda head, probs: probs_out.__setitem__((block, head), probs))
        mixed_out[:, at, :] = mixed.reshape(FRAMES, BLOCK, half)
        return carry

    lax.fori_loop(0, BLOCKS, third, 0)

    def fourth(step, carry):
        at = pl.ds(step * PAIR, PAIR)
        part = dot(flat(mixed_out[at]), outproj[...]).astype(LOW)
        part_out[at] = part.reshape(PAIR, ROWS, part.shape[1])
        return carry

    lax.fori_loop(0, FRAMES // PAIR, fourth, 0)


def heads_low(linear, inbias, half):
    query = ((linear[:, :half] + inbias[0:1]) * HEAD ** (-0.5)).astype(LOW)
    keys = linear[:, half : 2 * half].astype(LOW)
    values = (linear[:, 2 * half :] + inbias[1:2]).astype(LOW)
    return jnp.concatenate([query, keys, values], axis=1)


def beside(field_t, head):
    own = field_t[HEAD * head : HEAD * (head + 1)]
    none = jnp.zeros_like(own)
    return jnp.concatenate([own, none] if head % 2 == 0 else [none, own], axis=0)


def pair_of(field, head):
    start = head // 2 * 2 * HEAD
    return field[:, start : start + 2 * HEAD]


def attend(qkv, allowed, keep):
    half = qkv.shape[1] // 3
    query_t = qkv[:, :half].T
    keys = qkv[:, half : 2 * half]
    values_t = qkv[:, 2 * half :].T
    mixed_t = []
    for head in range(half // HEAD):
        scores = dot(pair_of(keys, head), beside(query_t, head))
        scores = jnp.where(allowed, scores, -1e30)
        expon = jnp.exp(scores - jnp.max(scores, axis=0, keepdims=True))
        probs = (expon * (1.0 / column_sum(expon))).astype(LOW)
        keep(head, probs)
        mixed_t.append(dot(values_t[HEAD * head : HEAD * (head + 1)], probs))
    return jnp.concatenate(mixed_t, axis=0).T.astype(LOW)


def attend_back(qkv, probs_of, d_mixed):
    half = qkv.shape[1] // 3
    query = qkv[:, :half]
    keys = qkv[:, half : 2 * half]
    keys_t = keys.T
    values = qkv[:, 2 * half :]
    d_mixed_t = d_mixed.T
    rows = qkv.shape[0]
    lane = iota((rows, 2 * HEAD), 1) < HEAD
    d_query_t = []
    d_keys = []
    d_values = []
    for head in range(half // HEAD):
        probs_low = probs_of(head)
        probs = wide(probs_low)
        d_probs = dot(pair_of(values, head), beside(d_mixed_t, head))
        inner = column_sum(probs * d_probs)
        d_scores = (probs * (d_probs - inner)).astype(LOW)
        d_values.append(dot(probs_low, pair_of(d_mixed, head)))
        d_keys.append(dot(d_scores, pair_of(query, head)))
        d_query_t.append(dot(keys_t[HEAD * head : HEAD * (head + 1)], d_scores))

    def paired(fields):
        return [jnp.where(lane, fields[at], fields[at + 1]) for at in range(0, len(fields), 2)]

    d_query = (jnp.concatenate(d_query_t, axis=0).T).astype(LOW) * HEAD ** (-0.5)
    return jnp.concatenate([d_query] + [d.astype(LOW) for d in paired(d_keys) + paired(d_values)], axis=1)


def time_forward(clips, gain, shift, inproj, inbias, outproj):
    tokens, width = clips.shape
    half = outproj.shape[0]
    heads = half // HEAD
    count = FRAMES * BLOCK
    args = (clips, gain, shift, inproj, inbias, outproj)
    outs = [
        shape((FRAMES, ROWS, width)),
        shape((FRAMES, ROWS, width)),
        shape((FRAMES, ROWS, 3 * half)),
        shape((BLOCKS, heads, count, count)),
        shape((FRAMES, ROWS, half)),
        shape((FRAMES, ROWS, width)),
    ]
    rows = FRAMES * ROWS
    return call(
        time_forward_kernel,
        (1,),
        [whole(a) for a in args],
        [whole(o) for o in outs],
        outs,
        [pltpu.VMEM((BLOCKS * count + BLOCK, width), LOW)],
        2 * rows * width * half * 5,
        args,
    )


def cotangent_kernel(cotangent, live, out, total, source):
    fill_rows(source, cotangent)
    present = live[0, 0]
    class_row = wide(cotangent[0:1])

    def first(block, carry):
        rows = frame_rows(source, block, class_row, 1) * present
        at = pl.ds(pl.multiple_of(block * BLOCK, BLOCK), BLOCK)
        out[:, at, :] = rows.astype(LOW).reshape(FRAMES, BLOCK, rows.shape[1])
        return carry + column_sum(rows)

    total[...] = lax.fori_loop(0, BLOCKS, first, jnp.zeros(total.shape, jnp.float32))


def cotangent_frames(cotangent, live):
    tokens, width = cotangent.shape
    args = (cotangent, live)
    outs = [shape((FRAMES, ROWS, width)), shape((1, width), jnp.float32)]
    return call(
        cotangent_kernel,
        (1,),
        [whole(cotangent), pl.BlockSpec(memory_space=pltpu.SMEM)],
        [whole(o) for o in outs],
        outs,
        [pltpu.VMEM((BLOCKS * FRAMES * BLOCK + BLOCK, width), LOW)],
        2 * FRAMES * ROWS * 128 * width,
        args,
    )


def place_of(shape_of):
    return iota(shape_of, 0) % ROWS


def space_forward_kernel(
    own, other, x, outbias, mixer, mixbias, gain, shift, inproj, inbias, outproj,
    mixer_out, after_out, norm_out, qkv_out, probs_out, mixed_out, part_out,
):
    half = outproj.shape[0]
    width = outproj.shape[1]

    def spread(field):
        return field.astype(LOW).reshape(PAIR, ROWS, field.shape[1])

    mixer_in = (wide(flat(own[...])) + wide(flat(other[...])) + outbias[...]).astype(LOW)
    mixer_out[...] = spread(mixer_in)
    branch = dot(mixer_in, mixer[...]) + mixbias[...]
    after = wide(flat(x[...])) + jnp.where(place_of((PAIR * ROWS, 1)) < PLACES, branch, 0.0)
    after_out[...] = spread(after)
    unit, _ = normed(after)
    norm = (unit * gain[...] + shift[...]).astype(LOW)
    norm_out[...] = spread(norm)
    qkv = heads_low(dot(norm, inproj[...]), inbias, half)
    qkv_out[...] = spread(qkv)
    allowed = iota((ROWS, ROWS), 0) <= PLACES
    for frame in range(PAIR):

        def keep(head, probs, frame=frame):
            probs_out[frame, head] = probs

        mixed_out[frame] = attend(qkv[frame * ROWS : (frame + 1) * ROWS], allowed, keep)
    part_out[...] = spread(dot(flat(mixed_out[...]), outproj[...]))


def pairs(array):
    rest = (0,) * (array.ndim - 1)
    return pl.BlockSpec((PAIR,) + array.shape[1:], lambda at: (at,) + rest)


def space_forward(own, other, x, outbias, mixer, mixbias, gain, shift, inproj, inbias, outproj):
    width = x.shape[2]
    half = outproj.shape[0]
    heads = half // HEAD
    args = (own, other, x, outbias, mixer, mixbias, gain, shift, inproj, inbias, outproj)
    outs = [
        shape((FRAMES, ROWS, width)),
        shape((FRAMES, ROWS, width)),
        shape((FRAMES, ROWS, width)),
        shape((FRAMES, ROWS, 3 * half)),
        shape((FRAMES, heads, ROWS, ROWS)),
        shape((FRAMES, ROWS, half)),
        shape((FRAMES, ROWS, width)),
    ]
    return call(
        space_forward_kernel,
        (FRAMES // PAIR,),
        [pairs(a) for a in args[:3]] + [whole(a) for a in args[3:]],
        [pairs(o) for o in outs],
        outs,
        [],
        2 * FRAMES * ROWS * width * half * 8,
        args,
    )


def last_block(count):
    return lambda array: pl.BlockSpec((count, BLOCK, array.shape[2]), lambda at: (0, BLOCKS - 1, 0))


CLASS_AT = PLACES - (BLOCKS - 1) * BLOCK


def feed_kernel(
    own, other, after, cot, own_last, other_last, after_last, outbias, gain, shift, upward, upbias, down,
    mid_out, norm_out, act_out, dpre_out, part_out, dnorm_out, upbias_out,
):
    step = pl.program_id(0)
    units = upward.shape[1]
    width = upward.shape[0]

    def spread(field):
        return field.astype(LOW).reshape(PAIR, ROWS, field.shape[1])

    class_branch = wide(own_last[...]) + wide(other_last[...])
    class_branch = jnp.sum(class_branch, axis=0)[CLASS_AT : CLASS_AT + 1] * (1.0 / FRAMES) + outbias[...]
    at = iota((PAIR * ROWS, 1), 0)
    branch = wide(flat(own[...])) + wide(flat(other[...])) + outbias[...]
    is_class = (at == PLACES) & (step == 0)
    mid = jnp.where(at % ROWS < PLACES, wide(flat(after[...])) + branch, 0.0)
    mid = mid + jnp.where(is_class, wide(after_last[0])[CLASS_AT : CLASS_AT + 1] + class_branch, 0.0)
    mid_out[...] = spread(mid)
    unit, _ = normed(mid)
    norm = (unit * gain[...] + shift[...]).astype(LOW)
    norm_out[...] = spread(norm)
    grad = flat(cot[...])
    part = jnp.zeros((PAIR * ROWS, width), jnp.float32)
    d_norm = jnp.zeros((PAIR * ROWS, width), jnp.float32)
    share = 512

    @pl.when(step == 0)
    def _():
        upbias_out[...] = jnp.zeros(upbias_out.shape, jnp.float32)

    for start in range(0, units, share):
        cols = slice(start, start + share)
        pre = dot(norm, upward[:, cols]) + upbias[:, cols]
        cumulative = 0.5 * (1.0 + lax.erf(pre * 0.5**0.5))
        slope = cumulative + pre * jnp.exp(-0.5 * pre * pre) * 0.3989422804014327
        act = (pre * cumulative).astype(LOW)
        act_out[:, :, cols] = spread(act)
        d_pre = (dot_last(grad, down[cols]) * slope).astype(LOW)
        dpre_out[:, :, cols] = spread(d_pre)
        upbias_out[:, cols] += column_sum(wide(d_pre))
        part = part + dot(act, down[cols])
        d_norm = d_norm + dot_last(d_pre, upward[:, cols])
    part_out[...] = spread(part)
    dnorm_out[...] = spread(d_norm)


def feed(own, other, after, cot, outbias, gain, shift, upward, upbias, down):
    width, units = upward.shape
    args = (own, other, after, cot, own, other, after, outbias, gain, shift, upward, upbias, down)
    outs = [
        shape((FRAMES, ROWS, width)),
        shape((FRAMES, ROWS, width)),
        shape((FRAMES, ROWS, units)),
        shape((FRAMES, ROWS, units)),
        shape((FRAMES, ROWS, width)),
        shape((FRAMES, ROWS, width)),
        shape((1, units), jnp.float32),
    ]
    tail = last_block(FRAMES)
    return call(
        feed_kernel,
        (FRAMES // PAIR,),
        [pairs(a) for a in args[:4]] + [tail(a) for a in args[4:7]] + [whole(a) for a in args[7:]],
        [pairs(o) for o in outs[:6]] + [whole(outs[6])],
        outs,
        [],
        2 * FRAMES * ROWS * width * units * 4,
        args,
    )


def space_backward_kernel(
    own, other, mid, cot, qkv, probs, own_last, other_last, mid_last, cot_last, gain, outproj, inproj,
    dspace_out, back_out, part_out, dclass_out, gain_out, shift_out, outbias_out, inbias_out,
):
    step = pl.program_id(0)
    half = outproj.shape[0]

    def spread(field):
        return field.astype(LOW).reshape(PAIR, ROWS, field.shape[1])

    def back(own_part, other_part, mid_part, cot_part):
        d_norm = wide(own_part) + wide(other_part)
        unit, inverse = normed(wide(mid_part))
        return wide(cot_part) + normed_back(unit, inverse, d_norm * gain[...]), d_norm, d_norm * unit

    d_class = back(own_last[0], other_last[0], mid_last[0], cot_last[0])[0][CLASS_AT : CLASS_AT + 1]
    d_mid, d_shift, d_gain = back(flat(own[...]), flat(other[...]), flat(mid[...]), flat(cot[...]))
    place = place_of((PAIR * ROWS, 1))
    d_space = jnp.where(place < PLACES, d_mid, jnp.where(place == PLACES, d_class * (1.0 / FRAMES), 0.0))

    @pl.when(step == 0)
    def _():
        dclass_out[...] = d_class
        for ref in (gain_out, shift_out, outbias_out, inbias_out):
            ref[...] = jnp.zeros(ref.shape, jnp.float32)

    gain_out[...] += column_sum(d_gain)
    shift_out[...] += column_sum(d_shift)
    outbias_out[...] += column_sum(d_space)
    d_low = d_space.astype(LOW)
    dspace_out[...] = spread(d_low)
    d_mixed = dot_last(d_low, outproj[...]).astype(LOW)
    for frame in range(PAIR):
        rows = slice(frame * ROWS, (frame + 1) * ROWS)
        back_out[frame] = attend_back(qkv[frame], lambda head, frame=frame: probs[frame, head], d_mixed[rows])
    backs = flat(back_out[...])
    inbias_out[...] += column_sum(wide(backs))
    part_out[...] = spread(dot_last(backs, inproj[...]))


def space_backward(own, other, mid, cot, qkv, probs, gain, outproj, inproj):
    width = mid.shape[2]
    half = outproj.shape[0]
    args = (own, other, mid, cot, qkv, probs, own, other, mid, cot, gain, outproj, inproj)
    outs = [
        shape((FRAMES, ROWS, width)),
        shape((FRAMES, ROWS, 3 * half)),
        shape((FRAMES, ROWS, width)),
        shape((1, width), jnp.float32),
        shape((1, width), jnp.float32),
        shape((1, width), jnp.float32),
        shape((1, width), jnp.float32),
        shape((1, 3 * half), jnp.float32),
    ]
    tail = last_block(1)
    return call(
        space_backward_kernel,
        (FRAMES // PAIR,),
        [pairs(a) for a in args[:6]] + [tail(a) for a in args[6:10]] + [whole(a) for a in args[10:]],
        [pairs(o) for o in outs[:3]] + [whole(o) for o in outs[3:]],
        outs,
        [],
        2 * FRAMES * ROWS * width * half * 6,
        args,
    )


def time_backward_kernel(
    own, other, after, dspace, dclass, qkv, probs, gain, mixer, outproj, inproj,
    dgrid_out, dmixer_out, back_out, part_out, dsource_out, gain_out, shift_out, mixbias_out, outbias_out, inbias_out,
    d_mixed,
):
    half = outproj.shape[0]
    width = outproj.shape[1]
    dsource_out[...] = dclass[...]
    for ref in (gain_out, shift_out, mixbias_out, outbias_out, inbias_out):
        ref[...] = jnp.zeros(ref.shape, jnp.float32)

    def first(step, carry):
        at = pl.ds(step * PAIR, PAIR)

        def put(ref, field):
            ref[at] = field.astype(LOW).reshape(PAIR, ROWS, field.shape[1])

        d_norm = wide(flat(own[at])) + wide(flat(other[at]))
        unit, inverse = normed(wide(flat(after[at])))
        gain_out[...] += column_sum(d_norm * unit)
        shift_out[...] += column_sum(d_norm)
        d_space_in = normed_back(unit, inverse, d_norm * gain[...])
        place = place_of((PAIR * ROWS, 1))
        dsource_out[...] += column_sum(jnp.where(place == PLACES, d_space_in, 0.0))
        d_grid = jnp.where(place < PLACES, d_space_in + wide(flat(dspace[at])), 0.0)
        mixbias_out[...] += column_sum(d_grid)
        d_low = d_grid.astype(LOW)
        put(dgrid_out, d_low)
        d_mixer = dot_last(d_low, mixer[...]).astype(LOW)
        put(dmixer_out, d_mixer)
        outbias_out[...] += column_sum(wide(d_mixer))
        put(d_mixed, dot_last(d_mixer, outproj[...]))
        return carry

    lax.fori_loop(0, FRAMES // PAIR, first, 0)

    def second(block, carry):
        at = pl.ds(pl.multiple_of(block * BLOCK, BLOCK), BLOCK)
        backs = attend_back(flat(qkv[:, at, :]), lambda head: probs[block, head], flat(d_mixed[:, at, :]))
        back_out[:, at, :] = backs.reshape(FRAMES, BLOCK, 3 * half)
        return carry

    lax.fori_loop(0, BLOCKS, second, 0)

    def third(step, carry):
        at = pl.ds(step * PAIR, PAIR)
        backs = flat(back_out[at])
        inbias_out[...] += column_sum(wide(backs))
        part_out[at] = dot_last(backs, inproj[...]).astype(LOW).reshape(PAIR, ROWS, width)
        return carry

    lax.fori_loop(0, FRAMES // PAIR, third, 0)


def time_backward(own, other, after, dspace, dclass, qkv, probs, gain, mixer, outproj, inproj):
    width = after.shape[2]
    half = outproj.shape[0]
    args = (own, other, after, dspace, dclass, qkv, probs, gain, mixer, outproj, inproj)
    outs = [
        shape((FRAMES, ROWS, width)),
        shape((FRAMES, ROWS, width)),
        shape((FRAMES, ROWS, 3 * half)),
        shape((FRAMES, ROWS, width)),
        shape((1, width), jnp.float32),
        shape((1, width), jnp.float32),
        shape((1, width), jnp.float32),
        shape((1, width), jnp.float32),
        shape((1, width), jnp.float32),
        shape((1, 3 * half), jnp.float32),
    ]
    return call(
        time_backward_kernel,
        (1,),
        [whole(a) for a in args],
        [whole(o) for o in outs],
        outs,
        [pltpu.VMEM((FRAMES, ROWS, half), LOW)],
        2 * FRAMES * ROWS * width * half * 8,
        args,
    )


def blocks(array):
    return pl.BlockSpec((FRAMES, BLOCK, array.shape[2]), lambda at: (0, at, 0))


def put_tokens(out, rows, carry):
    low = rows.astype(LOW)
    moved = to_tokens(low)
    out[...] = jnp.where(iota((rows.shape[0], 1), 0) == 0, carry[...], moved).astype(out.dtype)
    carry[...] = rows[rows.shape[0] - 1 :].astype(LOW).astype(jnp.float32)


def source_kernel(own, other, x, dgrid, dsource, gain, out, gain_out, shift_out, carry):
    block = pl.program_id(0)

    @pl.when(block == 0)
    def _():
        carry[...] = dsource[...]
        gain_out[...] = jnp.zeros(gain_out.shape, jnp.float32)
        shift_out[...] = jnp.zeros(shift_out.shape, jnp.float32)

    d_norm = wide(flat(own[...])) + wide(flat(other[...]))
    unit, inverse = normed(wide(flat(x[...])))
    gain_out[...] += column_sum(d_norm * unit)
    shift_out[...] += column_sum(d_norm)
    rows = wide(flat(dgrid[...])) + normed_back(unit, inverse, d_norm * gain[...])
    put_tokens(out, rows, carry)


def source_gradient(own, other, x, dgrid, dsource, gain, tokens):
    width = x.shape[2]
    args = (own, other, x, dgrid, dsource, gain)
    outs = [shape((tokens, width)), shape((1, width), jnp.float32), shape((1, width), jnp.float32)]
    out_block = pl.BlockSpec((FRAMES * BLOCK, width), lambda at: (at, 0))
    return call(
        source_kernel,
        (BLOCKS,),
        [blocks(a) for a in args[:4]] + [whole(a) for a in args[4:]],
        [out_block] + [whole(o) for o in outs[1:]],
        outs,
        [pltpu.VMEM((1, width), jnp.float32)],
        2 * FRAMES * ROWS * 128 * width,
        args,
    )


def result_kernel(own, other, mid, own_last, other_last, mid_last, bias, live, out, carry):
    present = live[0, 0]

    def rows_of(own_part, other_part, mid_part):
        return (wide(mid_part) + wide(own_part) + wide(other_part) + bias[...]) * present

    @pl.when(pl.program_id(0) == 0)
    def _():
        carry[...] = rows_of(own_last[0], other_last[0], mid_last[0])[CLASS_AT : CLASS_AT + 1]

    put_tokens(out, rows_of(flat(own[...]), flat(other[...]), flat(mid[...])), carry)


def result_tokens(own, other, mid, bias, live, tokens):
    width = mid.shape[2]
    args = (own, other, mid, own, other, mid, bias, live)
    tail = last_block(1)
    return call(
        result_kernel,
        (BLOCKS,),
        [blocks(a) for a in args[:3]] + [tail(a) for a in args[3:6]]
        + [whole(bias), pl.BlockSpec(memory_space=pltpu.SMEM)],
        [pl.BlockSpec((FRAMES * BLOCK, width), lambda at: (at, 0))],
        [shape((tokens, width))],
        [pltpu.VMEM((1, width), jnp.float32)],
        2 * FRAMES * ROWS * 128 * width,
        args,
    )[0]


def swap_tensor(field):
    size = lax.axis_size("tensor")
    return lax.ppermute(field, "tensor", [(i, i ^ 1) for i in range(size)])


def add_low(left, right):
    return (left.astype(jnp.float32) + right.astype(jnp.float32)).astype(jnp.bfloat16)


def halve(field, axis, bit, size, keep_bit):
    keep = lax.dynamic_index_in_dim(field, keep_bit, axis, keepdims=False)
    send = lax.dynamic_index_in_dim(field, 1 - keep_bit, axis, keepdims=False)
    got = lax.ppermute(send, "dp", [(i, i ^ bit) for i in range(size)])
    return add_low(keep, got)


def line_total(field, stride, size):
    count = field.shape[0]
    place = (lax.axis_index("dp") // stride) % count
    def at(offset):
        return lax.dynamic_index_in_dim(field, jnp.clip(place + offset, 0, count - 1), 0, keepdims=False)
    up = at(count - 1)
    down = at(1 - count)
    for step in range(1, count):
        ups = [(i, i + stride) for i in range(size) if (i // stride) % count < step and (i // stride) % count + 1 < count]
        downs = [(i, i - stride) for i in range(size) if (i // stride) % count > count - 1 - step]
        got_up = lax.ppermute(up, "dp", ups)
        got_down = lax.ppermute(down, "dp", downs)
        if step < count - 1:
            up = add_low(at(count - 1 - step), got_up)
            down = add_low(at(step + 1 - count), got_down)
    return (at(0).astype(jnp.float32) + got_up.astype(jnp.float32)) + got_down.astype(jnp.float32)


def dp_totals(first, second):
    size = lax.axis_size("dp")
    me = lax.axis_index("dp")
    if size == 16:
        def split(field):
            return field.reshape((4, 2, 2) + field.shape[1:])
        x_bit = me % 2
        y_bit = (me // 2) % 2
        first = halve(split(first), 2, 1, size, x_bit)
        second = halve(split(second), 1, 2, size, y_bit)
        first = halve(first, 1, 2, size, y_bit)
        second = halve(second, 1, 1, size, x_bit)
        return line_total(first, 4, size), line_total(second, 4, size)
    out = []
    for field in (first, second):
        span = size // 2
        while span >= 1:
            field = field.reshape((2, span) + field.shape[1:])
            field = halve(field, 0, span, size, (me // span) % 2)
            span //= 2
        out.append(field[0].astype(jnp.float32))
    return tuple(out)


def grad_of(left, right):
    return lax.dot_general(
        left.reshape(-1, left.shape[2]),
        right.reshape(-1, right.shape[2]),
        (((0,), (0,)), ((), ())),
        preferred_element_type=jnp.float32,
    ).astype(LOW)


def local(
    clips,
    cotangent,
    live,
    time_gain,
    time_shift,
    time_inproj,
    time_inbias,
    time_outproj,
    time_outbias,
    time_mixer,
    time_mixbias,
    space_gain,
    space_shift,
    space_inproj,
    space_inbias,
    space_outproj,
    space_outbias,
    feed_gain,
    feed_shift,
    feed_upward,
    feed_upbias,
    feed_down,
    feed_downbias,
):
    tokens, width = clips.shape[1:]
    half = time_outproj.shape[0]
    tensor_rank = lax.axis_index("tensor")
    present = live.astype(jnp.float32).reshape(1, 1)
    row = lambda vector: vector.reshape(1, -1)
    time_in = time_inproj.reshape(width, 3 * half)
    space_in = space_inproj.reshape(width, 3 * half)
    mixer_other = swap_tensor(time_mixer)
    mixer = jnp.where(
        tensor_rank == 0,
        jnp.concatenate([time_mixer, mixer_other], axis=0),
        jnp.concatenate([mixer_other, time_mixer], axis=0),
    )
    x, t_norm, t_qkv, t_probs, t_mixed, t_part = time_forward(
        clips[0], row(time_gain), row(time_shift), time_in, time_inbias, time_outproj
    )
    cot, g_downbias = cotangent_frames(cotangent[0], present)
    mixer_in, after, s_norm, s_qkv, s_probs, s_mixed, s_part = space_forward(
        t_part, swap_tensor(t_part), x, row(time_outbias), mixer, row(time_mixbias), row(space_gain),
        row(space_shift), space_in, space_inbias, space_outproj,
    )
    mid, f_norm, act, d_pre, f_part, df_part, g_upbias = feed(
        s_part, swap_tensor(s_part), after, cot, row(space_outbias), row(feed_gain), row(feed_shift), feed_upward,
        row(feed_upbias), feed_down,
    )
    g_up = grad_of(f_norm, d_pre)
    g_down = grad_of(cot, act)
    d_space, s_back, ds_part, d_class, g_feed_gain, g_feed_shift, g_space_outbias, g_space_inbias = space_backward(
        df_part, swap_tensor(df_part), mid, cot, s_qkv, s_probs, row(feed_gain), space_outproj, space_in
    )
    g_space_in = grad_of(s_norm, s_back)
    g_space_out = grad_of(d_space, s_mixed)
    (
        d_grid, d_mixer, t_back, dt_part, d_source, g_space_gain, g_space_shift, g_mixbias, g_outbias, g_time_inbias,
    ) = time_backward(
        ds_part, swap_tensor(ds_part), after, d_space, d_class, t_qkv, t_probs, row(space_gain), mixer, time_outproj,
        time_in,
    )
    mixer_half = lax.dynamic_slice_in_dim(mixer_in, tensor_rank * half, half, 2)
    g_mixer = grad_of(d_grid, mixer_half)
    g_time_out = grad_of(d_mixer, t_mixed)
    g_time_in = grad_of(t_norm, t_back)
    result = result_tokens(f_part, swap_tensor(f_part), mid, row(feed_downbias), present, tokens)
    grad_clips, g_time_gain, g_time_shift = source_gradient(
        dt_part, swap_tensor(dt_part), x, d_grid, d_source, row(time_gain), tokens
    )

    dests = lax.axis_size("dp")
    share = width // dests
    by_dest = lambda field: field.astype(LOW).reshape(dests, share, -1)
    up_sum, down_sum = dp_totals(by_dest(g_up), by_dest(g_down))
    space_a, space_b = dp_totals(
        by_dest(g_space_in[:, : 2 * half]),
        by_dest(jnp.concatenate([g_space_in[:, 2 * half :], g_space_out], axis=1)),
    )
    vectors = [
        g_time_gain, g_time_shift, g_outbias, g_mixbias, g_space_gain, g_space_shift, g_space_outbias, g_feed_gain,
        g_feed_shift, g_downbias, g_time_inbias[:, :half], g_time_inbias[:, 2 * half :], g_space_inbias[:, :half],
        g_space_inbias[:, 2 * half :], g_upbias,
    ]
    packed = jnp.concatenate([v.astype(LOW).reshape(dests, -1) for v in vectors], axis=1)
    packed = jnp.pad(packed, ((0, 0), (0, -packed.shape[1] % (2 * half)))).reshape(dests, -1, 2 * half)
    time_b = jnp.concatenate([g_time_out, g_mixer], axis=1).reshape(dests, share, 2 * half)
    time_a, time_b = dp_totals(by_dest(g_time_in), jnp.concatenate([time_b, packed], axis=1))
    loose = time_b[share:].reshape(-1)
    pieces = []
    at = 0
    for v in vectors:
        count = v.size // dests
        pieces.append(loose[at : at + count])
        at += count
    settled = (
        pieces[0],
        pieces[1],
        time_a.reshape(share, 3, half),
        jnp.stack([pieces[10], pieces[11]]),
        time_b[:share, :half].T,
        pieces[2],
        time_b[:share, half:].T,
        pieces[3],
        pieces[4],
        pieces[5],
        jnp.concatenate([space_a, space_b[:, :half]], axis=1).reshape(share, 3, half),
        jnp.stack([pieces[12], pieces[13]]),
        space_b[:, half:].T,
        pieces[6],
        pieces[7],
        pieces[8],
        up_sum,
        pieces[14],
        down_sum.T,
        pieces[9],
    )
    return (result[None], grad_clips[None]) + settled


def solution(mesh):
    in_specs = (
        P("dp", None, None),
        P("dp", None, None),
        P("dp"),
        P(),
        P(),
        P(None, None, "tensor"),
        P(None, "tensor"),
        P("tensor", None),
        P(),
        P("tensor", None),
        P(),
        P(),
        P(),
        P(None, None, "tensor"),
        P(None, "tensor"),
        P("tensor", None),
        P(),
        P(),
        P(),
        P(None, "tensor"),
        P("tensor"),
        P("tensor", None),
        P(),
    )
    out_specs = (
        P("dp", None, None),
        P("dp", None, None),
        P("dp"),
        P("dp"),
        P("dp", None, "tensor"),
        P(None, ("tensor", "dp")),
        P("tensor", "dp"),
        P("dp"),
        P("tensor", "dp"),
        P("dp"),
        P("dp"),
        P("dp"),
        P("dp", None, "tensor"),
        P(None, ("tensor", "dp")),
        P("tensor", "dp"),
        P("dp"),
        P("dp"),
        P("dp"),
        P("dp", "tensor"),
        P(("tensor", "dp")),
        P("tensor", "dp"),
        P("dp"),
    )
    return jax.shard_map(local, mesh=mesh, in_specs=in_specs, out_specs=out_specs, check_vma=False)
```

time: 713 us -> 454 us (0.64)
  Pallas kernels: 0 us -> 180 us
  matrix products: 192 us -> 30.8 us
  local copies, waits for them, and re-layouts: 184 us -> 33.4 us
  other arithmetic: 124 us -> 17 us
  waiting for transfers between devices: 97.9 us -> 79.7 us
    pallas_call x0 -> x8, Pallas kernels: none -> 180 us  [call(): pl.pallas_call(kernel, grid=grid, in_specs=in_specs, out_specs=out_specs,...]
    dot_general x33 -> x7, matrix products: 192 us -> 30.8 us  [grad_of(): lax.dot_general(left.reshape(-1, left.shape[2]), right.reshape(-1, right....]
    convert_element_type x26 -> x0, local copies, waits for them, and re-layouts: 57.3 us -> none  [the longest x2 6.88 us: time_inproj_back(): values_low = d_values.reshape(flat).astype(jnp.bfloat16)]
    reduce_sum x17 -> x0, other arithmetic: 49.4 us -> none  [the longest x4 23.1 us: layer_norm(): return center * lax.rsqrt(spread_sq + 1e-06) * gain + shift]
    slice x18 -> x7, local copies, waits for them, and re-layouts: 30.2 us -> 2.01 us  [the longest x3 1.27 us: local(): pieces.append(loose[at:at + count])]
    convert_element_type x8 -> x7, other arithmetic: 27.2 us -> 3.51 us  [local(): v.astype(LOW).reshape(dests, -1)]
    dot_general x4 -> x0, local copies, waits for them, and re-layouts: 19.2 us -> none  [the longest x2 12.3 us: time_inproj_back(): jnp.einsum('pfd,cfkp->dck', normed, stacked, preferred_element_type=jnp.f...]
    add x7 -> x0, other arithmetic: 13.7 us -> none  [the longest x1 5.05 us: branch_total(): return low.astype(jnp.float32) + other.astype(jnp.float32)]
  transfers between devices with their start and end apart: 56 -> 55, of which waited for: 19 -> 16; matrix products, arithmetic and copies ran while one was open for 17% -> 14% of each run, Pallas kernels for 0% -> 14%
where the time goes in v2:
time: 454 us; the launch traced here: 446 us
  Pallas kernels  180 us (40%)
  starting transfers between devices  102 us (22%)
  waiting for transfers between devices  79.7 us (18%)
  local copies, waits for them, and re-layouts  33.4 us (7%)
  matrix products  30.8 us (7%)
  other arithmetic  17 us (4%)
    pallas_call x8, Pallas kernels, call(): pl.pallas_call(kernel, grid=grid, in_specs=in_specs, out_specs=out_specs,...  180 us
    ppermute x18, starting transfers between devices, line_total(): got_up = lax.ppermute(up, 'dp', ups)  67.2 us
    ppermute x12, waiting for transfers between devices, halve(): got = lax.ppermute(send, 'dp', [(i, i ^ bit) for i in range(size)])  57.9 us
    dot_general x7, matrix products, grad_of(): lax.dot_general(left.reshape(-1, left.shape[2]), right.reshape(-1, right....  30.8 us
    ppermute x18, waiting for transfers between devices, line_total(): got_down = lax.ppermute(down, 'dp', downs)  17.7 us
    ppermute x12, starting transfers between devices, halve(): got = lax.ppermute(send, 'dp', [(i, i ^ bit) for i in range(size)])  17.2 us
    ppermute x18, starting transfers between devices, line_total(): got_down = lax.ppermute(down, 'dp', downs)  15.8 us
  transfers between devices with their start and end apart: 55, of which 16 were waited for; matrix products, arithmetic and copies ran while one was open for 14% of the time, Pallas kernels for 14%

profile of v2, /device:TPU:0, one launch (start us, length us, event | category | flops | bytes accessed | tf_op | source)
XLA Modules:
  0.0 445.8 jit_solution(16615026535685817113)
XLA Ops:
  0.7 2.6 copy.98
  3.3 2.2 copy.99.inproj
  6.7 26.2 %shard_map.390 = (bf16[8,208,768]{2,1,0:T(8,128)(2,1)}, bf16[8,208,768]{2,1,0:T(8,128)(2,1)}, bf16[8,208,1152]{2,1,0:T(8,128)(2,1)}, bf16[13,6,128,128]{3,2,1,0:...) custom-call(bf16[1569,768]{1,0:T(8,128)(2,1)} %bitcast.296, f32[1,768]{1,0:T(1,128)} %reshape.265.gain, ...), custom_call_target="tpu_custom_call" | custom-call | flops 4907335680 | bytes 20113920 | tf_op jit(solution)/shard_map/pallas_call | solution.py:61
  34.4 2.2 copy.101.inproj
  38.9 2.9 maximum_select_fusion.mixer
  41.9 27.6 %shard_map.391 = (bf16[8,208,768]{2,1,0:T(8,128)(2,1)}, bf16[8,208,768]{2,1,0:T(8,128)(2,1)}, bf16[8,208,768]{2,1,0:T(8,128)(2,1)}, bf16[8,208,1152]{2,1,0:T(8,1...) custom-call(bf16[8,208,768]{2,1,0:T(8,128)(2,1)} %get-tuple-element.65.own, ...), custom_call_target="tpu_custom_call" | custom-call | flops 7851737088 | bytes 30710784 | tf_op jit(solution)/shard_map/pallas_call | solution.py:61
  73.0 6.2 %shard_map.392 = (bf16[8,208,768]{2,1,0:T(8,128)(2,1)}, f32[1,768]{1,0:T(1,128)}) custom-call(bf16[1569,768]{1,0:T(8,128)(2,1)} %bitcast.285, f32[1,1]{1,0:T(1,128)} %bitcast.4.live), custom_call_target="tpu_custom_call" | custom-call | flops 327155712 | bytes 4968964 | tf_op jit(solution)/shard_map/pallas_call | solution.py:61
  79.2 1.5 copy-done.25
  80.7 26.7 %shard_map.393 = (bf16[8,208,768]{2,1,0:T(8,128)(2,1)}, bf16[8,208,768]{2,1,0:T(8,128)(2,1)}, bf16[8,208,1536]{2,1,0:T(8,128)(2,1)}, bf16[8,208,1536]{2,1,0:T(8,...) custom-call(bf16[8,208,768]{2,1,0:T(8,128)(2,1)} %get-tuple-element.67.own.own_last, ...), custom_call_target="tpu_custom_call" | custom-call | flops 15703474176 | bytes 43078656 | tf_op jit(solution)/shard_map/pallas_call | solution.py:61
  107.4 7.3 %bitcast_convert_fusion = bf16[768,1536]{1,0:T(8,128)(2,1)S(1)} fusion(bf16[8,208,768]{2,1,0:T(8,128)(2,1)S(1)} %copy-done, bf16[8,208,1536]{2,1,0:T(8,128)(2,1)} %get-tuple-element.107), kind=kOutput, calls=%fused_computation | convolution fusion | flops 3927048192 | bytes 10027008 | tf_op jit(solution)/shard_map/dot_general | solution.py:709
  117.1 2.6 collective-permute-start.47
  119.7 4.8 %bitcast_convert_fusion.1 = bf16[768,1536]{1,0:T(8,128)(2,1)S(1)} fusion(bf16[8,208,768]{2,1,0:T(8,128)(2,1)S(1)} %copy-done.30, bf16[8,208,1536]{2,1,0:T(8,128)(2,1)S(1)} %copy-done.27), kind=kOutput, calls=%fused_computation.1 | convolution fusion | flops 3927048192 | bytes 10027008 | tf_op jit(solution)/shard_map/dot_general | solution.py:709
  126.9 1.5 collective-permute-start.39
  129.8 16.8 %collective-permute-done.47 = bf16[4,2,48,1536]{3,2,0,1:T(8,128)(2,1)} collective-permute-done((bf16[4,2,48,1536]{3,2,0,1:T(8,128)(2,1)}, bf16[4,2,48,1536]{3,2,0,1:T(8,128)(2,1)}, u32[]{:S(2)}, u32[]{:S(2)}) %collective-permute-start.47) | collective-permute-done | bytes 1179680 | tf_op jit(solution)/shard_map/ppermute | solution.py:662
  146.6 2.0 fusion.2
  148.7 1.8 collective-permute-start.48
  150.4 5.6 %collective-permute-done.39 = bf16[4,2,48,1536]{3,2,0,1:T(8,128)(2,1)} collective-permute-done((bf16[4,2,48,1536]{3,2,0,1:T(8,128)(2,1)}, bf16[4,2,48,1536]{3,2,0,1:T(8,128)(2,1)}, u32[]{:S(2)}, u32[]{:S(2)}) %collective-permute-start.39) | collective-permute-done | bytes 1179680 | tf_op jit(solution)/shard_map/ppermute | solution.py:662
  156.1 1.6 fusion.3
  158.6 9.2 %collective-permute-done.48 = bf16[4,48,1536]{2,1,0:T(8,128)(2,1)S(1)} collective-permute-done((bf16[4,48,1536]{2,1,0:T(8,128)(2,1)S(1)}, bf16[4,48,1536]{2,1,0:T(8,128)(2,1)S(1)}, u32[]{:S(2)}, u32[]{:S(2)}) %collective-permute-start.48) | collective-permute-done | bytes 589856 | tf_op jit(solution)/shard_map/ppermute | solution.py:662
  168.0 3.5 collective-permute-start.49
  172.4 2.8 collective-permute-start.41
  176.0 1.9 collective-permute-done.41
  177.9 4.4 collective-permute-start.50
  182.3 1.9 collective-permute-start.42
  185.9 5.0 %collective-permute-start.51 = (bf16[48,1536]{1,0:T(8,128)(2,1)S(1)}, bf16[48,1536]{1,0:T(8,128)(2,1)S(1)}, u32[]{:S(2)}, u32[]{:S(2)}) collective-permute-start(bf16[48,1536]{1,0:T(8,128)(2,1)S(1)} %get-tuple-element.188), channel_id=1, source_target_pairs={{0,8},{2,10},{4,12},{6,14},{8,16},{10,18},{12,20},{14,22},{16,24},... | collective-permute-start | bytes 442376 | tf_op jit(solution)/shard_map/ppermute | solution.py:676
  191.7 5.9 %collective-permute-start.43 = (bf16[48,1536]{1,0:T(8,128)(2,1)S(1)}, bf16[48,1536]{1,0:T(8,128)(2,1)S(1)}, u32[]{:S(2)}, u32[]{:S(2)}) collective-permute-start(bf16[48,1536]{1,0:T(8,128)(2,1)S(1)} %get-tuple-element.192), channel_id=1, source_target_pairs={{0,8},{2,10},{4,12},{6,14},{8,16},{10,18},{12,20},{14,22},{16,24},... | collective-permute-start | bytes 442376 | tf_op jit(solution)/shard_map/ppermute | solution.py:676
  197.7 1.3 collective-permute-start.54
  200.3 5.4 %collective-permute-done.54 = bf16[48,1536]{1,0:T(8,128)(2,1)S(1)} collective-permute-done((bf16[48,1536]{1,0:T(8,128)(2,1)S(1)}, bf16[48,1536]{1,0:T(8,128)(2,1)S(1)}, u32[]{:S(2)}, u32[]{:S(2)}) %collective-permute-start.54) | collective-permute-done | bytes 147488 | tf_op jit(solution)/shard_map/ppermute | solution.py:677
  208.5 29.5 %shard_map.395 = (bf16[8,208,768]{2,1,0:T(8,128)(2,1)}, bf16[8,208,1152]{2,1,0:T(8,128)(2,1)}, bf16[8,208,768]{2,1,0:T(8,128)(2,1)}, f32[1,768]{1,0:T(1,128)}, f...) custom-call(bf16[8,208,768]{2,1,0:T(8,128)(2,1)} %get-tuple-element.72.own.own_last, ...), custom_call_target="tpu_custom_call" | custom-call | flops 5888802816 | bytes 39759360 | tf_op jit(solution)/shard_map/pallas_call | solution.py:61
  238.1 5.8 %fusion.1 = bf16[768,1152]{1,0:T(8,128)(2,1)S(1)} fusion(bf16[8,208,768]{2,1,0:T(8,128)(2,1)S(1)} %copy-done.28, bf16[8,208,1152]{2,1,0:T(8,128)(2,1)} %get-tuple-element.103), kind=kOutput, calls=%fused_computation.5 | convolution fusion | flops 2945286144 | bytes 8159232 | tf_op jit(solution)/shard_map/dot_general | solution.py:709
  244.2 1.5 collective-permute-start.23
  246.1 1.6 fusion.8
  249.4 1.5 collective-permute-start.31
  253.6 1.4 reshape.285
  255.0 10.8 %shard_map.394 = bf16[1569,768]{1,0:T(8,128)(2,1)} custom-call(bf16[8,208,768]{2,1,0:T(8,128)(2,1)} %get-tuple-element.70.own.own_last, bf16[8,208,768]{2,1,0:T(8,128)(2,1)} %collective-permute-done.3.other.other_last, bf16[8,208,768]{2,1,0:T(8,128)(2,1)} %get-tuple-element.71.mid.mid_last, bf16[8,208,768]{2,1,0:T(8,128)(2,1)} %get-tuple-element.70.own.own_last, ...), custom_call_target="tpu_custom_call" | custom-call | flops 327155712 | bytes 17748484 | tf_op jit(solution)/shard_map/pallas_call | solution.py:61
  266.8 1.5 collective-permute-start.32
  268.4 6.8 %collective-permute-done.24 = bf16[4,48,768]{2,1,0:T(8,128)(2,1)S(1)} collective-permute-done((bf16[4,48,768]{2,1,0:T(8,128)(2,1)S(1)}, bf16[4,48,768]{2,1,0:T(8,128)(2,1)S(1)}, u32[]{:S(2)}, u32[]{:S(2)}) %collective-permute-start.24) | collective-permute-done | bytes 294944 | tf_op jit(solution)/shard_map/ppermute | solution.py:662
  275.3 3.9 collective-permute-start.25
  280.0 1.3 collective-permute-start.33
  282.0 4.0 collective-permute-start.26
  286.0 1.9 collective-permute-start.34
  289.0 5.0 %collective-permute-start.27 = (bf16[48,768]{1,0:T(8,128)(2,1)S(1)}, bf16[48,768]{1,0:T(8,128)(2,1)S(1)}, u32[]{:S(2)}, u32[]{:S(2)}) collective-permute-start(bf16[48,768]{1,0:T(8,128)(2,1)S(1)} %get-tuple-element.204), channel_id=1, source_target_pairs={{0,8},{2,10},{4,12},{6,14},{8,16},{10,18},{12,20},{14,22},{16,24},... | collective-permute-start | bytes 221192 | tf_op jit(solution)/shard_map/ppermute | solution.py:676
  294.7 5.2 %collective-permute-start.35 = (bf16[48,768]{1,0:T(8,128)(2,1)S(1)}, bf16[48,768]{1,0:T(8,128)(2,1)S(1)}, u32[]{:S(2)}, u32[]{:S(2)}) collective-permute-start(bf16[48,768]{1,0:T(8,128)(2,1)S(1)} %get-tuple-element.208), channel_id=1, source_target_pairs={{0,8},{2,10},{4,12},{6,14},{8,16},{10,18},{12,20},{14,22},{16,24},... | collective-permute-start | bytes 221192 | tf_op jit(solution)/shard_map/ppermute | solution.py:676
  301.3 1.3 collective-permute-start.38
  302.6 4.2 collective-permute-done.30
  306.9 1.9 collective-permute-done.38
  308.8 39.5 %shard_map.396 = (bf16[8,208,768]{2,1,0:T(8,128)(2,1)}, bf16[8,208,768]{2,1,0:T(8,128)(2,1)}, bf16[8,208,1152]{2,1,0:T(8,128)(2,1)}, bf16[8,208,768]{2,1,0:T(8,1...) custom-call(bf16[8,208,768]{2,1,0:T(8,128)(2,1)} %get-tuple-element., ...), custom_call_target="tpu_custom_call" | custom-call | flops 7851737088 | bytes 31680000 | tf_op jit(solution)/shard_map/pallas_call | solution.py:61
  351.5 6.6 %fusion = bf16[768,1152]{1,0:T(8,128)(2,1)S(1)} fusion(bf16[8,208,768]{2,1,0:T(8,128)(2,1)} %get-tuple-element.100, bf16[8,208,1152]{2,1,0:T(8,128)(2,1)} %get-tuple-element.101), kind=kOutput, calls=%fused_computation.4 | convolution fusion | flops 2945286144 | bytes 8159232 | tf_op jit(solution)/shard_map/dot_general | solution.py:709
  359.3 1.5 collective-permute-start.15
  361.0 1.3 fusion.7
  362.5 3.4 fusion.6
  366.7 13.9 %shard_map.397 = (bf16[1569,768]{1,0:T(8,128)(2,1)}, f32[1,768]{1,0:T(1,128)}, f32[1,768]{1,0:T(1,128)}) custom-call(bf16[8,208,768]{2,1,0:T(8,128)(2,1)} %get-tuple-element.80.own, bf16[8,208,768]{2,1,0:T(8,128)(2,1)} %collective-permute-done.6.other, bf16[8,208,768]{2,1,0:T(8,128)(2,1)} %get-tuple-element.66.x, ...), custom_call_target="tpu_custom_call" | custom-call | flops 327155712 | bytes 12645888 | tf_op jit(solution)/shard_map/pallas_call | solution.py:61
  382.7 1.4 fusion.4
  384.1 1.5 collective-permute-start.16
  386.3 12.1 %collective-permute-done.7 = bf16[4,2,49,768]{3,0,2,1:T(4,128)(2,1)S(1)} collective-permute-done((bf16[4,2,49,768]{3,0,2,1:T(4,128)(2,1)S(1)}, bf16[4,2,49,768]{3,0,2,1:T(4,128)(2,1)S(1)}, u32[]{:S(2)}, u32[]{:S(2)}) %collective-permute-start.7) | collective-permute-done | bytes 602144 | tf_op jit(solution)/shard_map/ppermute | solution.py:662
  398.7 1.5 collective-permute-start.8
  400.2 7.4 %collective-permute-done.16 = bf16[4,48,1152]{2,1,0:T(8,128)(2,1)S(1)} collective-permute-done((bf16[4,48,1152]{2,1,0:T(8,128)(2,1)S(1)}, bf16[4,48,1152]{2,1,0:T(8,128)(2,1)S(1)}, u32[]{:S(2)}, u32[]{:S(2)}) %collective-permute-start.16) | collective-permute-done | bytes 442400 | tf_op jit(solution)/shard_map/ppermute | solution.py:662
  407.7 3.9 collective-permute-start.17
  412.5 1.3 collective-permute-start.9
  414.3 4.4 collective-permute-start.18
  419.4 1.9 collective-permute-start.10
  422.5 5.0 %collective-permute-start.19 = (bf16[48,1152]{1,0:T(8,128)(2,1)S(1)}, bf16[48,1152]{1,0:T(8,128)(2,1)S(1)}, u32[]{:S(2)}, u32[]{:S(2)}) collective-permute-start(bf16[48,1152]{1,0:T(8,128)(2,1)S(1)} %get-tuple-element.196), channel_id=1, source_target_pairs={{0,8},{2,10},{4,12},{6,14},{8,16},{10,18},{12,20},{14,22},{16,24},... | collective-permute-start | bytes 331784 | tf_op jit(solution)/shard_map/ppermute | solution.py:676
  429.6 5.8 %collective-permute-start.11 = (bf16[49,768]{1,0:T(8,128)(2,1)S(1)}, bf16[49,768]{1,0:T(8,128)(2,1)S(1)}, u32[]{:S(2)}, u32[]{:S(2)}) collective-permute-start(bf16[49,768]{1,0:T(8,128)(2,1)S(1)} %get-tuple-element.200), channel_id=1, source_target_pairs={{0,8},{2,10},{4,12},{6,14},{8,16},{10,18},{12,20},{14,22},{16,24},... | collective-permute-start | bytes 225800 | tf_op jit(solution)/shard_map/ppermute | solution.py:676
  437.5 4.9 %collective-permute-done.14 = bf16[49,768]{1,0:T(8,128)(2,1)S(1)} collective-permute-done((bf16[49,768]{1,0:T(8,128)(2,1)S(1)}, bf16[49,768]{1,0:T(8,128)(2,1)S(1)}, u32[]{:S(2)}, u32[]{:S(2)}) %collective-permute-start.14) | collective-permute-done | bytes 75296 | tf_op jit(solution)/shard_map/ppermute | solution.py:677
  (243 shorter events, 53.1 us)
Async XLA Ops:
  6.7 26.7 %copy-start.4 = (bf16[768,3,384]{2,0,1:T(8,128)(2,1)S(1)}, bf16[768,3,384]{2,0,1:T(8,128)(2,1)}, u32[]{:S(2)}) copy-start(bf16[768,3,384]{2,0,1:T(8,128)(2,1)} %param.36) | copy-start | bytes 5308420
  32.9 9.0 %collective-permute-start = (bf16[8,208,768]{2,1,0:T(8,128)(2,1)}, bf16[8,208,768]{2,1,0:T(8,128)(2,1)}, u32[]{:S(2)}, u32[]{:S(2)}) collective-permute-start(bf16[8,208,768]{2,1,0:T(8,128)(2,1)} %get-tuple-element.65.own), channel_id=1, source_target_pairs={{0,1},{1,0},{2,3},{3,2},{4,5},{5,4},{6,7},{7,6},{8,9},{9,8},{10,11... | collective-permute-start | bytes 7667720 | tf_op jit(solution)/shard_map/ppermute | solution.py:652
  33.3 5.6 %collective-permute-start.1 = (bf16[384,768]{1,0:T(8,128)(2,1)}, bf16[384,768]{1,0:T(8,128)(2,1)}, u32[]{:S(2)}, u32[]{:S(2)}) collective-permute-start(bf16[384,768]{1,0:T(8,128)(2,1)} %param.32), channel_id=1, source_target_pairs={{0,1},{1,0},{2,3},{3,2},{4,5},{5,4},{6,7},{7,6},{8,9},{9,8},{10,11... | collective-permute-start | bytes 1769480 | tf_op jit(solution)/shard_map/ppermute | solution.py:652
  41.9 28.7 %copy-start.17 = (f32[768]{0:T(1024)S(1)}, f32[768]{0:T(1024)}, u32[]{:S(2)}) copy-start(f32[768]{0:T(1024)} %param.40) | copy-start | bytes 9220
  41.9 29.3 %copy-start.8 = (f32[1536]{0:T(1024)S(1)}, f32[1536]{0:T(1024)}, u32[]{:S(2)}) copy-start(f32[1536]{0:T(1024)} %param.43) | copy-start | bytes 18436
  41.9 29.9 %copy-start.18 = (f32[768]{0:T(1024)S(1)}, f32[768]{0:T(1024)}, u32[]{:S(2)}) copy-start(f32[768]{0:T(1024)} %param.39) | copy-start | bytes 9220
  41.9 30.5 %copy-start.19 = (f32[768]{0:T(1024)S(1)}, f32[768]{0:T(1024)}, u32[]{:S(2)}) copy-start(f32[768]{0:T(1024)} %param.41) | copy-start | bytes 9220
  69.5 9.7 %collective-permute-start.2 = (bf16[8,208,768]{2,1,0:T(8,128)(2,1)}, bf16[8,208,768]{2,1,0:T(8,128)(2,1)S(1)}, u32[]{:S(2)}, u32[]{:S(2)}) collective-permute-start(bf16[8,208,768]{2,1,0:T(8,128)(2,1)} %get-tuple-element.67.own.own_last), channel_id=1, source_target_pairs={{0,1},{1,0},{2,3},{3,2},{4,5},{5,4},{6,7},{7,6},{8,9},{9,8},{10,11... | collective-permute-start | bytes 7667720 | tf_op jit(solution)/shard_map/ppermute | solution.py:652
  80.7 26.7 %copy-start = (bf16[8,208,768]{2,1,0:T(8,128)(2,1)S(1)}, bf16[8,208,768]{2,1,0:T(8,128)(2,1)}, u32[]{:S(2)}) copy-start(bf16[8,208,768]{2,1,0:T(8,128)(2,1)} %get-tuple-element.69.cot.cot_last) | copy-start | bytes 7667716
  117.1 29.5 %collective-permute-start.47 = (bf16[4,2,48,1536]{3,2,0,1:T(8,128)(2,1)}, bf16[4,2,48,1536]{3,2,0,1:T(8,128)(2,1)}, u32[]{:S(2)}, u32[]{:S(2)}) collective-permute-start(bf16[4,2,48,1536]{3,2,0,1:T(8,128)(2,1)} %bitcast.272), channel_id=1, source_target_pairs={{0,4},{2,6},{4,0},{6,2},{8,12},{10,14},{12,8},{14,10},{16,20},{18,... | collective-permute-start | bytes 3538952 | tf_op jit(solution)/shard_map/ppermute | solution.py:662
  126.9 29.1 %collective-permute-start.39 = (bf16[4,2,48,1536]{3,2,0,1:T(8,128)(2,1)}, bf16[4,2,48,1536]{3,2,0,1:T(8,128)(2,1)}, u32[]{:S(2)}, u32[]{:S(2)}) collective-permute-start(bf16[4,2,48,1536]{3,2,0,1:T(8,128)(2,1)} %bitcast.273), channel_id=1, source_target_pairs={{0,2},{2,0},{4,6},{6,4},{8,10},{10,8},{12,14},{14,12},{16,18},{18,... | collective-permute-start | bytes 3538952 | tf_op jit(solution)/shard_map/ppermute | solution.py:662
  129.1 79.4 %collective-permute-start.4 = (bf16[8,208,768]{2,1,0:T(8,128)(2,1)S(1)}, bf16[8,208,768]{2,1,0:T(8,128)(2,1)}, u32[]{:S(2)}, u32[]{:S(2)}) collective-permute-start(bf16[8,208,768]{2,1,0:T(8,128)(2,1)S(1)} %copy-done.1), channel_id=1, source_target_pairs={{0,1},{1,0},{2,3},{3,2},{4,5},{5,4},{6,7},{7,6},{8,9},{9,8},{10,11... | collective-permute-start | bytes 7667720 | tf_op jit(solution)/shard_map/ppermute | solution.py:652
  129.3 125.7 %collective-permute-start.3 = (bf16[8,208,768]{2,1,0:T(8,128)(2,1)}, bf16[8,208,768]{2,1,0:T(8,128)(2,1)}, u32[]{:S(2)}, u32[]{:S(2)}) collective-permute-start(bf16[8,208,768]{2,1,0:T(8,128)(2,1)} %get-tuple-element.70.own.own_last), channel_id=1, source_target_pairs={{0,1},{1,0},{2,3},{3,2},{4,5},{5,4},{6,7},{7,6},{8,9},{9,8},{10,11... | collective-permute-start | bytes 7667720 | tf_op jit(solution)/shard_map/ppermute | solution.py:652
  148.7 19.2 %collective-permute-start.48 = (bf16[4,48,1536]{2,1,0:T(8,128)(2,1)S(1)}, bf16[4,48,1536]{2,1,0:T(8,128)(2,1)S(1)}, u32[]{:S(2)}, u32[]{:S(2)}) collective-permute-start(bf16[4,48,1536]{2,1,0:T(8,128)(2,1)S(1)} %dynamic-slice_bitcast_fusion), channel_id=1, source_target_pairs={{0,2},{2,0},{4,6},{6,4},{8,10},{10,8},{12,14},{14,12},{16,18},{18,... | collective-permute-start | bytes 1769480 | tf_op jit(solution)/shard_map/ppermute | solution.py:662
  157.7 14.5 %collective-permute-start.40 = (bf16[4,48,1536]{2,1,0:T(8,128)(2,1)S(1)}, bf16[4,48,1536]{2,1,0:T(8,128)(2,1)S(1)}, u32[]{:S(2)}, u32[]{:S(2)}) collective-permute-start(bf16[4,48,1536]{2,1,0:T(8,128)(2,1)S(1)} %dynamic-slice_bitcast_fusion.1), channel_id=1, source_target_pairs={{0,4},{2,6},{4,0},{6,2},{8,12},{10,14},{12,8},{14,10},{16,20},{18,... | collective-permute-start | bytes 1769480 | tf_op jit(solution)/shard_map/ppermute | solution.py:662
  168.0 7.2 %collective-permute-start.49 = (bf16[48,1536]{1,0:T(8,128)(2,1)S(1)}, bf16[48,1536]{1,0:T(8,128)(2,1)S(1)}, u32[]{:S(2)}, u32[]{:S(2)}) collective-permute-start(bf16[48,1536]{1,0:T(8,128)(2,1)S(1)} %get-tuple-element.190), channel_id=1, source_target_pairs={{0,8},{2,10},{4,12},{6,14},{1,9},{3,11},{5,13},{7,15}} | collective-permute-start | bytes 442376 | tf_op jit(solution)/shard_map/ppermute | solution.py:676
  171.5 10.8 %collective-permute-start.52 = (bf16[48,1536]{1,0:T(8,128)(2,1)S(1)}, bf16[48,1536]{1,0:T(8,128)(2,1)S(1)}, u32[]{:S(2)}, u32[]{:S(2)}) collective-permute-start(bf16[48,1536]{1,0:T(8,128)(2,1)S(1)} %get-tuple-element.191), channel_id=1, source_target_pairs={{24,16},{26,18},{28,20},{30,22},{25,17},{27,19},{29,21},{31,23}} | collective-permute-start | bytes 442376 | tf_op jit(solution)/shard_map/ppermute | solution.py:677
  172.4 5.5 %collective-permute-start.41 = (bf16[48,1536]{1,0:T(8,128)(2,1)S(1)}, bf16[48,1536]{1,0:T(8,128)(2,1)S(1)}, u32[]{:S(2)}, u32[]{:S(2)}) collective-permute-start(bf16[48,1536]{1,0:T(8,128)(2,1)S(1)} %get-tuple-element.194), channel_id=1, source_target_pairs={{0,8},{2,10},{4,12},{6,14},{1,9},{3,11},{5,13},{7,15}} | collective-permute-start | bytes 442376 | tf_op jit(solution)/shard_map/ppermute | solution.py:676
  175.3 10.7 %collective-permute-start.44 = (bf16[48,1536]{1,0:T(8,128)(2,1)S(1)}, bf16[48,1536]{1,0:T(8,128)(2,1)S(1)}, u32[]{:S(2)}, u32[]{:S(2)}) collective-permute-start(bf16[48,1536]{1,0:T(8,128)(2,1)S(1)} %get-tuple-element.195), channel_id=1, source_target_pairs={{24,16},{26,18},{28,20},{30,22},{25,17},{27,19},{29,21},{31,23}} | collective-permute-start | bytes 442376 | tf_op jit(solution)/shard_map/ppermute | solution.py:677
  177.9 7.3 %collective-permute-start.50 = (bf16[48,1536]{1,0:T(8,128)(2,1)S(1)}, bf16[48,1536]{1,0:T(8,128)(2,1)S(1)}, u32[]{:S(2)}, u32[]{:S(2)}) collective-permute-start(bf16[48,1536]{1,0:T(8,128)(2,1)S(1)} %fusion.24), channel_id=1, source_target_pairs={{0,8},{2,10},{4,12},{6,14},{8,16},{10,18},{12,20},{14,22},{1,9},{3... | collective-permute-start | bytes 442376 | tf_op jit(solution)/shard_map/ppermute | solution.py:676
  182.3 8.6 %collective-permute-start.42 = (bf16[48,1536]{1,0:T(8,128)(2,1)S(1)}, bf16[48,1536]{1,0:T(8,128)(2,1)S(1)}, u32[]{:S(2)}, u32[]{:S(2)}) collective-permute-start(bf16[48,1536]{1,0:T(8,128)(2,1)S(1)} %fusion.30), channel_id=1, source_target_pairs={{0,8},{2,10},{4,12},{6,14},{8,16},{10,18},{12,20},{14,22},{1,9},{3... | collective-permute-start | bytes 442376 | tf_op jit(solution)/shard_map/ppermute | solution.py:676
  185.2 6.5 %collective-permute-start.53 = (bf16[48,1536]{1,0:T(8,128)(2,1)S(1)}, bf16[48,1536]{1,0:T(8,128)(2,1)S(1)}, u32[]{:S(2)}, u32[]{:S(2)}) collective-permute-start(bf16[48,1536]{1,0:T(8,128)(2,1)S(1)} %get-tuple-element.189), channel_id=1, source_target_pairs={{16,8},{18,10},{20,12},{22,14},{24,16},{26,18},{28,20},{30,22},{17... | collective-permute-start | bytes 442376 | tf_op jit(solution)/shard_map/ppermute | solution.py:677
  185.9 13.1 %collective-permute-start.51 = (bf16[48,1536]{1,0:T(8,128)(2,1)S(1)}, bf16[48,1536]{1,0:T(8,128)(2,1)S(1)}, u32[]{:S(2)}, u32[]{:S(2)}) collective-permute-start(bf16[48,1536]{1,0:T(8,128)(2,1)S(1)} %get-tuple-element.188), channel_id=1, source_target_pairs={{0,8},{2,10},{4,12},{6,14},{8,16},{10,18},{12,20},{14,22},{16,24},... | collective-permute-start | bytes 442376 | tf_op jit(solution)/shard_map/ppermute | solution.py:676
  191.1 6.6 %collective-permute-start.45 = (bf16[48,1536]{1,0:T(8,128)(2,1)S(1)}, bf16[48,1536]{1,0:T(8,128)(2,1)S(1)}, u32[]{:S(2)}, u32[]{:S(2)}) collective-permute-start(bf16[48,1536]{1,0:T(8,128)(2,1)S(1)} %get-tuple-element.193), channel_id=1, source_target_pairs={{16,8},{18,10},{20,12},{22,14},{24,16},{26,18},{28,20},{30,22},{17... | collective-permute-start | bytes 442376 | tf_op jit(solution)/shard_map/ppermute | solution.py:677
  191.7 14.8 %collective-permute-start.43 = (bf16[48,1536]{1,0:T(8,128)(2,1)S(1)}, bf16[48,1536]{1,0:T(8,128)(2,1)S(1)}, u32[]{:S(2)}, u32[]{:S(2)}) collective-permute-start(bf16[48,1536]{1,0:T(8,128)(2,1)S(1)} %get-tuple-element.192), channel_id=1, source_target_pairs={{0,8},{2,10},{4,12},{6,14},{8,16},{10,18},{12,20},{14,22},{16,24},... | collective-permute-start | bytes 442376 | tf_op jit(solution)/shard_map/ppermute | solution.py:676
  197.7 8.1 %collective-permute-start.54 = (bf16[48,1536]{1,0:T(8,128)(2,1)S(1)}, bf16[48,1536]{1,0:T(8,128)(2,1)S(1)}, u32[]{:S(2)}, u32[]{:S(2)}) collective-permute-start(bf16[48,1536]{1,0:T(8,128)(2,1)S(1)} %fusion.23), channel_id=1, source_target_pairs={{8,0},{10,2},{12,4},{14,6},{16,8},{18,10},{20,12},{22,14},{24,16},... | collective-permute-start | bytes 442376 | tf_op jit(solution)/shard_map/ppermute | solution.py:677
  199.0 8.7 %collective-permute-start.46 = (bf16[48,1536]{1,0:T(8,128)(2,1)S(1)}, bf16[48,1536]{1,0:T(8,128)(2,1)S(1)}, u32[]{:S(2)}, u32[]{:S(2)}) collective-permute-start(bf16[48,1536]{1,0:T(8,128)(2,1)S(1)} %fusion.29), channel_id=1, source_target_pairs={{8,0},{10,2},{12,4},{14,6},{16,8},{18,10},{20,12},{22,14},{24,16},... | collective-permute-start | bytes 442376 | tf_op jit(solution)/shard_map/ppermute | solution.py:677
  208.5 29.6 %copy-start.28 = (bf16[8,208,768]{2,1,0:T(8,128)(2,1)S(1)}, bf16[8,208,768]{2,1,0:T(8,128)(2,1)}, u32[]{:S(2)}) copy-start(bf16[8,208,768]{2,1,0:T(8,128)(2,1)} %get-tuple-element.102) | copy-start | bytes 7667716
  238.0 70.8 %collective-permute-start.5 = (bf16[8,208,768]{2,1,0:T(8,128)(2,1)}, bf16[8,208,768]{2,1,0:T(8,128)(2,1)}, u32[]{:S(2)}, u32[]{:S(2)}) collective-permute-start(bf16[8,208,768]{2,1,0:T(8,128)(2,1)} %get-tuple-element.75.own), channel_id=1, source_target_pairs={{0,1},{1,0},{2,3},{3,2},{4,5},{5,4},{6,7},{7,6},{8,9},{9,8},{10,11... | collective-permute-start | bytes 7667720 | tf_op jit(solution)/shard_map/ppermute | solution.py:652
  244.2 21.7 %collective-permute-start.23 = (bf16[4,2,48,768]{3,2,0,1:T(8,128)(2,1)S(1)}, bf16[4,2,48,768]{3,2,0,1:T(8,128)(2,1)S(1)}, u32[]{:S(2)}, u32[]{:S(2)}) collective-permute-start(bf16[4,2,48,768]{3,2,0,1:T(8,128)(2,1)S(1)} %bitcast.292), channel_id=1, source_target_pairs={{0,2},{2,0},{4,6},{6,4},{8,10},{10,8},{12,14},{14,12},{16,18},{18,... | collective-permute-start | bytes 1769480 | tf_op jit(solution)/shard_map/ppermute | solution.py:662
  249.4 17.2 %collective-permute-start.31 = (bf16[4,2,48,768]{3,2,0,1:T(8,128)(2,1)S(1)}, bf16[4,2,48,768]{3,2,0,1:T(8,128)(2,1)S(1)}, u32[]{:S(2)}, u32[]{:S(2)}) collective-permute-start(bf16[4,2,48,768]{3,2,0,1:T(8,128)(2,1)S(1)} %bitcast.293), channel_id=1, source_target_pairs={{0,4},{2,6},{4,0},{6,2},{8,12},{10,14},{12,8},{14,10},{16,20},{18,... | collective-permute-start | bytes 1769480 | tf_op jit(solution)/shard_map/ppermute | solution.py:662
  266.0 9.2 %collective-permute-start.24 = (bf16[4,48,768]{2,1,0:T(8,128)(2,1)S(1)}, bf16[4,48,768]{2,1,0:T(8,128)(2,1)S(1)}, u32[]{:S(2)}, u32[]{:S(2)}) collective-permute-start(bf16[4,48,768]{2,1,0:T(8,128)(2,1)S(1)} %dynamic-slice_bitcast_fusion.5), channel_id=1, source_target_pairs={{0,4},{2,6},{4,0},{6,2},{8,12},{10,14},{12,8},{14,10},{16,20},{18,... | collective-permute-start | bytes 884744 | tf_op jit(solution)/shard_map/ppermute | solution.py:662
  266.8 13.1 %collective-permute-start.32 = (bf16[4,48,768]{2,1,0:T(8,128)(2,1)S(1)}, bf16[4,48,768]{2,1,0:T(8,128)(2,1)S(1)}, u32[]{:S(2)}, u32[]{:S(2)}) collective-permute-start(bf16[4,48,768]{2,1,0:T(8,128)(2,1)S(1)} %dynamic-slice_bitcast_fusion.4), channel_id=1, source_target_pairs={{0,2},{2,0},{4,6},{6,4},{8,10},{10,8},{12,14},{14,12},{16,18},{18,... | collective-permute-start | bytes 884744 | tf_op jit(solution)/shard_map/ppermute | solution.py:662
  275.3 6.7 %collective-permute-start.25 = (bf16[48,768]{1,0:T(8,128)(2,1)S(1)}, bf16[48,768]{1,0:T(8,128)(2,1)S(1)}, u32[]{:S(2)}, u32[]{:S(2)}) collective-permute-start(bf16[48,768]{1,0:T(8,128)(2,1)S(1)} %get-tuple-element.206), channel_id=1, source_target_pairs={{0,8},{2,10},{4,12},{6,14},{1,9},{3,11},{5,13},{7,15}} | collective-permute-start | bytes 221192 | tf_op jit(solution)/shard_map/ppermute | solution.py:676
  279.2 8.8 %collective-permute-start.28 = (bf16[48,768]{1,0:T(8,128)(2,1)S(1)}, bf16[48,768]{1,0:T(8,128)(2,1)S(1)}, u32[]{:S(2)}, u32[]{:S(2)}) collective-permute-start(bf16[48,768]{1,0:T(8,128)(2,1)S(1)} %get-tuple-element.207), channel_id=1, source_target_pairs={{24,16},{26,18},{28,20},{30,22},{25,17},{27,19},{29,21},{31,23}} | collective-permute-start | bytes 221192 | tf_op jit(solution)/shard_map/ppermute | solution.py:677
  280.0 6.0 %collective-permute-start.33 = (bf16[48,768]{1,0:T(8,128)(2,1)S(1)}, bf16[48,768]{1,0:T(8,128)(2,1)S(1)}, u32[]{:S(2)}, u32[]{:S(2)}) collective-permute-start(bf16[48,768]{1,0:T(8,128)(2,1)S(1)} %get-tuple-element.210), channel_id=1, source_target_pairs={{0,8},{2,10},{4,12},{6,14},{1,9},{3,11},{5,13},{7,15}} | collective-permute-start | bytes 221192 | tf_op jit(solution)/shard_map/ppermute | solution.py:676
  281.3 12.7 %collective-permute-start.36 = (bf16[48,768]{1,0:T(8,128)(2,1)S(1)}, bf16[48,768]{1,0:T(8,128)(2,1)S(1)}, u32[]{:S(2)}, u32[]{:S(2)}) collective-permute-start(bf16[48,768]{1,0:T(8,128)(2,1)S(1)} %get-tuple-element.211), channel_id=1, source_target_pairs={{24,16},{26,18},{28,20},{30,22},{25,17},{27,19},{29,21},{31,23}} | collective-permute-start | bytes 221192 | tf_op jit(solution)/shard_map/ppermute | solution.py:677
  282.0 6.2 %collective-permute-start.26 = (bf16[48,768]{1,0:T(8,128)(2,1)S(1)}, bf16[48,768]{1,0:T(8,128)(2,1)S(1)}, u32[]{:S(2)}, u32[]{:S(2)}) collective-permute-start(bf16[48,768]{1,0:T(8,128)(2,1)S(1)} %fusion.50), channel_id=1, source_target_pairs={{0,8},{2,10},{4,12},{6,14},{8,16},{10,18},{12,20},{14,22},{1,9},{3... | collective-permute-start | bytes 221192 | tf_op jit(solution)/shard_map/ppermute | solution.py:676
  286.0 7.9 %collective-permute-start.34 = (bf16[48,768]{1,0:T(8,128)(2,1)S(1)}, bf16[48,768]{1,0:T(8,128)(2,1)S(1)}, u32[]{:S(2)}, u32[]{:S(2)}) collective-permute-start(bf16[48,768]{1,0:T(8,128)(2,1)S(1)} %fusion.45), channel_id=1, source_target_pairs={{0,8},{2,10},{4,12},{6,14},{8,16},{10,18},{12,20},{14,22},{1,9},{3... | collective-permute-start | bytes 221192 | tf_op jit(solution)/shard_map/ppermute | solution.py:676
  288.3 11.6 %collective-permute-start.29 = (bf16[48,768]{1,0:T(8,128)(2,1)S(1)}, bf16[48,768]{1,0:T(8,128)(2,1)S(1)}, u32[]{:S(2)}, u32[]{:S(2)}) collective-permute-start(bf16[48,768]{1,0:T(8,128)(2,1)S(1)} %get-tuple-element.205), channel_id=1, source_target_pairs={{16,8},{18,10},{20,12},{22,14},{24,16},{26,18},{28,20},{30,22},{17... | collective-permute-start | bytes 221192 | tf_op jit(solution)/shard_map/ppermute | solution.py:677
  289.0 13.6 %collective-permute-start.27 = (bf16[48,768]{1,0:T(8,128)(2,1)S(1)}, bf16[48,768]{1,0:T(8,128)(2,1)S(1)}, u32[]{:S(2)}, u32[]{:S(2)}) collective-permute-start(bf16[48,768]{1,0:T(8,128)(2,1)S(1)} %get-tuple-element.204), channel_id=1, source_target_pairs={{0,8},{2,10},{4,12},{6,14},{8,16},{10,18},{12,20},{14,22},{16,24},... | collective-permute-start | bytes 221192 | tf_op jit(solution)/shard_map/ppermute | solution.py:676
  294.0 7.2 %collective-permute-start.37 = (bf16[48,768]{1,0:T(8,128)(2,1)S(1)}, bf16[48,768]{1,0:T(8,128)(2,1)S(1)}, u32[]{:S(2)}, u32[]{:S(2)}) collective-permute-start(bf16[48,768]{1,0:T(8,128)(2,1)S(1)} %get-tuple-element.209), channel_id=1, source_target_pairs={{16,8},{18,10},{20,12},{22,14},{24,16},{26,18},{28,20},{30,22},{17... | collective-permute-start | bytes 221192 | tf_op jit(solution)/shard_map/ppermute | solution.py:677
  294.7 12.1 %collective-permute-start.35 = (bf16[48,768]{1,0:T(8,128)(2,1)S(1)}, bf16[48,768]{1,0:T(8,128)(2,1)S(1)}, u32[]{:S(2)}, u32[]{:S(2)}) collective-permute-start(bf16[48,768]{1,0:T(8,128)(2,1)S(1)} %get-tuple-element.208), channel_id=1, source_target_pairs={{0,8},{2,10},{4,12},{6,14},{8,16},{10,18},{12,20},{14,22},{16,24},... | collective-permute-start | bytes 221192 | tf_op jit(solution)/shard_map/ppermute | solution.py:676
  299.9 6.9 %collective-permute-start.30 = (bf16[48,768]{1,0:T(8,128)(2,1)S(1)}, bf16[48,768]{1,0:T(8,128)(2,1)S(1)}, u32[]{:S(2)}, u32[]{:S(2)}) collective-permute-start(bf16[48,768]{1,0:T(8,128)(2,1)S(1)} %fusion.49), channel_id=1, source_target_pairs={{8,0},{10,2},{12,4},{14,6},{16,8},{18,10},{20,12},{22,14},{24,16},... | collective-permute-start | bytes 221192 | tf_op jit(solution)/shard_map/ppermute | solution.py:677
  301.3 7.5 %collective-permute-start.38 = (bf16[48,768]{1,0:T(8,128)(2,1)S(1)}, bf16[48,768]{1,0:T(8,128)(2,1)S(1)}, u32[]{:S(2)}, u32[]{:S(2)}) collective-permute-start(bf16[48,768]{1,0:T(8,128)(2,1)S(1)} %fusion.44), channel_id=1, source_target_pairs={{8,0},{10,2},{12,4},{14,6},{16,8},{18,10},{20,12},{22,14},{24,16},... | collective-permute-start | bytes 221192 | tf_op jit(solution)/shard_map/ppermute | solution.py:677
  348.3 18.3 %collective-permute-start.6 = (bf16[8,208,768]{2,1,0:T(8,128)(2,1)}, bf16[8,208,768]{2,1,0:T(8,128)(2,1)}, u32[]{:S(2)}, u32[]{:S(2)}) collective-permute-start(bf16[8,208,768]{2,1,0:T(8,128)(2,1)} %get-tuple-element.80.own), channel_id=1, source_target_pairs={{0,1},{1,0},{2,3},{3,2},{4,5},{5,4},{6,7},{7,6},{8,9},{9,8},{10,11... | collective-permute-start | bytes 7667720 | tf_op jit(solution)/shard_map/ppermute | solution.py:652
  359.3 23.4 %collective-permute-start.15 = (bf16[4,2,48,1152]{3,2,0,1:T(8,128)(2,1)}, bf16[4,2,48,1152]{3,2,0,1:T(8,128)(2,1)}, u32[]{:S(2)}, u32[]{:S(2)}) collective-permute-start(bf16[4,2,48,1152]{3,2,0,1:T(8,128)(2,1)} %bitcast.274), channel_id=1, source_target_pairs={{0,2},{2,0},{4,6},{6,4},{8,10},{10,8},{12,14},{14,12},{16,18},{18,... | collective-permute-start | bytes 2654216 | tf_op jit(solution)/shard_map/ppermute | solution.py:662
  366.6 14.8 %copy-start.5 = (bf16[16,48]{1,0:T(8,128)(2,1)S(1)}, bf16[16,48]{1,0:T(8,128)(2,1)}, u32[]{:S(2)}) copy-start(bf16[16,48]{1,0:T(8,128)(2,1)} %reshape.286) | copy-start | bytes 4612
  366.6 14.8 %copy-start.6 = (bf16[16,48]{1,0:T(8,128)(2,1)S(1)}, bf16[16,48]{1,0:T(8,128)(2,1)}, u32[]{:S(2)}) copy-start(bf16[16,48]{1,0:T(8,128)(2,1)} %reshape.287) | copy-start | bytes 4612
  382.0 16.5 %collective-permute-start.7 = (bf16[4,2,49,768]{3,0,2,1:T(4,128)(2,1)S(1)}, bf16[4,2,49,768]{3,0,2,1:T(4,128)(2,1)S(1)}, u32[]{:S(2)}, u32[]{:S(2)}) collective-permute-start(bf16[4,2,49,768]{3,0,2,1:T(4,128)(2,1)S(1)} %copy.107), channel_id=1, source_target_pairs={{0,4},{2,6},{4,0},{6,2},{8,12},{10,14},{12,8},{14,10},{16,20},{18,... | collective-permute-start | bytes 1806344 | tf_op jit(solution)/shard_map/ppermute | solution.py:662
  384.1 23.5 %collective-permute-start.16 = (bf16[4,48,1152]{2,1,0:T(8,128)(2,1)S(1)}, bf16[4,48,1152]{2,1,0:T(8,128)(2,1)S(1)}, u32[]{:S(2)}, u32[]{:S(2)}) collective-permute-start(bf16[4,48,1152]{2,1,0:T(8,128)(2,1)S(1)} %dynamic-slice_bitcast_fusion.2), channel_id=1, source_target_pairs={{0,4},{2,6},{4,0},{6,2},{8,12},{10,14},{12,8},{14,10},{16,20},{18,... | collective-permute-start | bytes 1327112 | tf_op jit(solution)/shard_map/ppermute | solution.py:662
  398.7 13.7 %collective-permute-start.8 = (bf16[4,49,768]{2,1,0:T(8,128)(2,1)S(1)}, bf16[4,49,768]{2,1,0:T(8,128)(2,1)S(1)}, u32[]{:S(2)}, u32[]{:S(2)}) collective-permute-start(bf16[4,49,768]{2,1,0:T(8,128)(2,1)S(1)} %dynamic-slice_bitcast_fusion.3), channel_id=1, source_target_pairs={{0,2},{2,0},{4,6},{6,4},{8,10},{10,8},{12,14},{14,12},{16,18},{18,... | collective-permute-start | bytes 903176 | tf_op jit(solution)/shard_map/ppermute | solution.py:662
  407.7 6.5 %collective-permute-start.17 = (bf16[48,1152]{1,0:T(8,128)(2,1)S(1)}, bf16[48,1152]{1,0:T(8,128)(2,1)S(1)}, u32[]{:S(2)}, u32[]{:S(2)}) collective-permute-start(bf16[48,1152]{1,0:T(8,128)(2,1)S(1)} %get-tuple-element.198), channel_id=1, source_target_pairs={{0,8},{2,10},{4,12},{6,14},{1,9},{3,11},{5,13},{7,15}} | collective-permute-start | bytes 331784 | tf_op jit(solution)/shard_map/ppermute | solution.py:676
  411.7 9.7 %collective-permute-start.20 = (bf16[48,1152]{1,0:T(8,128)(2,1)S(1)}, bf16[48,1152]{1,0:T(8,128)(2,1)S(1)}, u32[]{:S(2)}, u32[]{:S(2)}) collective-permute-start(bf16[48,1152]{1,0:T(8,128)(2,1)S(1)} %get-tuple-element.199), channel_id=1, source_target_pairs={{24,16},{26,18},{28,20},{30,22},{25,17},{27,19},{29,21},{31,23}} | collective-permute-start | bytes 331784 | tf_op jit(solution)/shard_map/ppermute | solution.py:677
  412.5 6.9 %collective-permute-start.9 = (bf16[49,768]{1,0:T(8,128)(2,1)S(1)}, bf16[49,768]{1,0:T(8,128)(2,1)S(1)}, u32[]{:S(2)}, u32[]{:S(2)}) collective-permute-start(bf16[49,768]{1,0:T(8,128)(2,1)S(1)} %get-tuple-element.202), channel_id=1, source_target_pairs={{0,8},{2,10},{4,12},{6,14},{1,9},{3,11},{5,13},{7,15}} | collective-permute-start | bytes 225800 | tf_op jit(solution)/shard_map/ppermute | solution.py:676
  414.3 7.5 %collective-permute-start.18 = (bf16[48,1152]{1,0:T(8,128)(2,1)S(1)}, bf16[48,1152]{1,0:T(8,128)(2,1)S(1)}, u32[]{:S(2)}, u32[]{:S(2)}) collective-permute-start(bf16[48,1152]{1,0:T(8,128)(2,1)S(1)} %fusion.35), channel_id=1, source_target_pairs={{0,8},{2,10},{4,12},{6,14},{8,16},{10,18},{12,20},{14,22},{1,9},{3... | collective-permute-start | bytes 331784 | tf_op jit(solution)/shard_map/ppermute | solution.py:676
  418.7 8.8 %collective-permute-start.12 = (bf16[49,768]{1,0:T(8,128)(2,1)S(1)}, bf16[49,768]{1,0:T(8,128)(2,1)S(1)}, u32[]{:S(2)}, u32[]{:S(2)}) collective-permute-start(bf16[49,768]{1,0:T(8,128)(2,1)S(1)} %get-tuple-element.203), channel_id=1, source_target_pairs={{24,16},{26,18},{28,20},{30,22},{25,17},{27,19},{29,21},{31,23}} | collective-permute-start | bytes 225800 | tf_op jit(solution)/shard_map/ppermute | solution.py:677
  419.4 8.1 %collective-permute-start.10 = (bf16[49,768]{1,0:T(8,128)(2,1)S(1)}, bf16[49,768]{1,0:T(8,128)(2,1)S(1)}, u32[]{:S(2)}, u32[]{:S(2)}) collective-permute-start(bf16[49,768]{1,0:T(8,128)(2,1)S(1)} %fusion.40), channel_id=1, source_target_pairs={{0,8},{2,10},{4,12},{6,14},{8,16},{10,18},{12,20},{14,22},{1,9},{3... | collective-permute-start | bytes 225800 | tf_op jit(solution)/shard_map/ppermute | solution.py:676
  421.8 6.5 %collective-permute-start.21 = (bf16[48,1152]{1,0:T(8,128)(2,1)S(1)}, bf16[48,1152]{1,0:T(8,128)(2,1)S(1)}, u32[]{:S(2)}, u32[]{:S(2)}) collective-permute-start(bf16[48,1152]{1,0:T(8,128)(2,1)S(1)} %get-tuple-element.197), channel_id=1, source_target_pairs={{16,8},{18,10},{20,12},{22,14},{24,16},{26,18},{28,20},{30,22},{17... | collective-permute-start | bytes 331784 | tf_op jit(solution)/shard_map/ppermute | solution.py:677
  422.5 14.3 %collective-permute-start.19 = (bf16[48,1152]{1,0:T(8,128)(2,1)S(1)}, bf16[48,1152]{1,0:T(8,128)(2,1)S(1)}, u32[]{:S(2)}, u32[]{:S(2)}) collective-permute-start(bf16[48,1152]{1,0:T(8,128)(2,1)S(1)} %get-tuple-element.196), channel_id=1, source_target_pairs={{0,8},{2,10},{4,12},{6,14},{8,16},{10,18},{12,20},{14,22},{16,24},... | collective-permute-start | bytes 331784 | tf_op jit(solution)/shard_map/ppermute | solution.py:676
  427.6 7.8 %collective-permute-start.13 = (bf16[49,768]{1,0:T(8,128)(2,1)S(1)}, bf16[49,768]{1,0:T(8,128)(2,1)S(1)}, u32[]{:S(2)}, u32[]{:S(2)}) collective-permute-start(bf16[49,768]{1,0:T(8,128)(2,1)S(1)} %get-tuple-element.201), channel_id=1, source_target_pairs={{16,8},{18,10},{20,12},{22,14},{24,16},{26,18},{28,20},{30,22},{17... | collective-permute-start | bytes 225800 | tf_op jit(solution)/shard_map/ppermute | solution.py:677
  428.3 8.5 %collective-permute-start.22 = (bf16[48,1152]{1,0:T(8,128)(2,1)S(1)}, bf16[48,1152]{1,0:T(8,128)(2,1)S(1)}, u32[]{:S(2)}, u32[]{:S(2)}) collective-permute-start(bf16[48,1152]{1,0:T(8,128)(2,1)S(1)} %fusion.34), channel_id=1, source_target_pairs={{8,0},{10,2},{12,4},{14,6},{16,8},{18,10},{20,12},{22,14},{24,16},... | collective-permute-start | bytes 331784 | tf_op jit(solution)/shard_map/ppermute | solution.py:677
  429.6 7.9 %collective-permute-start.11 = (bf16[49,768]{1,0:T(8,128)(2,1)S(1)}, bf16[49,768]{1,0:T(8,128)(2,1)S(1)}, u32[]{:S(2)}, u32[]{:S(2)}) collective-permute-start(bf16[49,768]{1,0:T(8,128)(2,1)S(1)} %get-tuple-element.200), channel_id=1, source_target_pairs={{0,8},{2,10},{4,12},{6,14},{8,16},{10,18},{12,20},{14,22},{16,24},... | collective-permute-start | bytes 225800 | tf_op jit(solution)/shard_map/ppermute | solution.py:676
  435.5 7.0 %collective-permute-start.14 = (bf16[49,768]{1,0:T(8,128)(2,1)S(1)}, bf16[49,768]{1,0:T(8,128)(2,1)S(1)}, u32[]{:S(2)}, u32[]{:S(2)}) collective-permute-start(bf16[49,768]{1,0:T(8,128)(2,1)S(1)} %fusion.39), channel_id=1, source_target_pairs={{8,0},{10,2},{12,4},{14,6},{16,8},{18,10},{20,12},{22,14},{24,16},... | collective-permute-start | bytes 225800 | tf_op jit(solution)/shard_map/ppermute | solution.py:677
  (22 other events, 89.8 us)
